TPU v7x, 512 devices: a whole 4x8x8 slice. The times are simulated.
512 devices in a mesh: gx: 16 (over y, core), gy: 8 (over x, z_hi), gz: 4 (over z_lo).
Axes of the slice: x: 4, y: 8, z: 8 (z_hi: 2, z_lo: 4; z = z_hi * 4 + z_lo), core: 2. Of those that a mesh axis runs over, the one named last changes fastest.
Arguments:
- upper: float32 [64, 128, 1024], P('gz', 'gx', 'gy'), as said below
- lower: float32 [64, 128, 1024], P('gz', 'gx', 'gy')
- velocity: float32 [3, 64, 128, 1024], P(None, 'gz', 'gx', 'gy'), may hold values from -0.25 to 0.25
- diffusivity: float32 [64, 128, 1024], P('gz', 'gx', 'gy'), may hold values from 0.004 to 0.04
- sensor_center: float32 [4, 16384, 1024], P('gz', ('gx', 'gy')), may hold values from -6 to 6
- sensor_error: float32 [4, 16384], P('gz', ('gx', 'gy')), may hold values from 0.05 to 0.5
- sensor_block: int32 [4, 16384], P('gz', ('gx', 'gy')), may hold values from 0 to 2047, as said below
Outputs:
- upper_out: float32 [64, 128, 1024], P('gz', 'gx', 'gy')
- lower_out: float32 [64, 128, 1024], P('gz', 'gx', 'gy')
Inputs may be any that keep to these rules, and one draw needn't show every extreme that they name: `sensor_block`: each entry names a block of the layer of its row (see the steps). In the entries of one device (aligned runs of 128 entries) at most 2 blocks lie on any one device of the layer; in every layer some device holds exactly 2 footprints from every device of the layer. Every entry of upper minus lower is positive.
All inputs are finite; a program needn't handle non-finite values.
Results may differ from a plain program's by a relative error of at most 0.00002.
Values sent between devices are 32-bit elements; how exact they have to be, the bound alone decides.
A program may use at most 64 MiB of HBM per device.

v0:
```python
import jax
import jax.numpy as jnp
from jax import lax
from jax.sharding import PartitionSpec as P


def with_halo(cells, sides, width):
    for axis, dim in sides:
        count = lax.axis_size(axis)
        ends = count - 1
        head = lax.slice_in_dim(cells, 0, width, axis=dim)
        tail = lax.slice_in_dim(cells, cells.shape[dim] - width, cells.shape[dim], axis=dim)
        cells = jnp.concatenate(
            [
                lax.ppermute(tail, axis, [(i, (i + 1) % count) for i in range(ends)]),
                cells,
                lax.ppermute(head, axis, [((i + 1) % count, i) for i in range(ends)]),
            ],
            axis=dim,
        )
    return cells


def take(field, dim, offset):
    index = [slice(None)]
    for axis in range(1, 4):
        length = field.shape[axis]
        if axis == dim:
            index.append(slice(1 + offset, length - 1 + offset))
        else:
            index.append(slice(1, length - 1))
    return field[tuple(index)]


def advance(padded, coeffs):
    center = take(padded, 1, 0)
    middle = take(coeffs, 1, 0)
    result = center
    nearby = jnp.zeros_like(center)
    for comp in range(3):
        below = take(padded, comp + 1, -1)
        above = take(padded, comp + 1, 1)
        speed_below = take(coeffs, comp + 1, -1)[comp]
        speed_above = take(coeffs, comp + 1, 1)[comp]
        result = (
            result
            - jnp.abs(middle[comp]) * center
            + jnp.maximum(speed_below, 0.0) * below
            + jnp.maximum(-speed_above, 0.0) * above
        )
        nearby = nearby + below + above
    return result + middle[3] * (nearby - 6.0 * center)


def to_blocks(field):
    depth, rows, cols = field.shape
    cut = field.reshape(depth // 16, 16, rows // 8, 8, cols // 8, 8)
    return cut.transpose(0, 2, 4, 1, 3, 5).reshape(-1, 1024)


def from_blocks(blocks, depth, rows, cols):
    cut = blocks.reshape(depth // 16, rows // 8, cols // 8, 16, 8, 8)
    return cut.transpose(0, 3, 1, 4, 2, 5).reshape(depth, rows, cols)


def shards(upper, lower, velocity, diffusivity, sensor_center, sensor_error, sensor_block):
    depth, rows, cols = upper.shape
    size_x = lax.axis_size("gx")
    size_y = lax.axis_size("gy")
    owners = size_x * size_y
    blocks = sensor_block[0]
    count = blocks.shape[0]
    cap = max(2, 2 * count // owners)
    along_x = rows // 8
    along_y = cols // 8
    wide_y = cols * size_y // 8
    wide_x = rows * size_x // 8
    level = blocks // (wide_x * wide_y)
    within = blocks % (wide_x * wide_y)
    block_x = within // wide_y
    block_y = within % wide_y
    owner = block_x // along_x * size_y + block_y // along_y
    local = level * along_x * along_y + block_x % along_x * along_y + block_y % along_y
    onehot = (owner[:, None] == jnp.arange(owners, dtype=jnp.int32)[None, :]).astype(jnp.int32)
    rank = jnp.sum((jnp.cumsum(onehot, axis=0) - onehot) * onehot, axis=1)
    position = owner * cap + rank
    outgoing = jnp.zeros((owners * cap, 1024), jnp.float32).at[position].set(sensor_center[0])
    margins = jnp.zeros((owners * cap,), jnp.float32).at[position].set(sensor_error[0])
    labels = (
        jnp.full((owners * cap,), -1.0, jnp.float32).at[position].set(local.astype(jnp.float32))
    )
    got_center, got_error, got_label = (
        lax.all_to_all(
            outgoing.reshape(owners, cap, 1024),
            ("gx", "gy"),
            split_axis=0,
            concat_axis=0,
            tiled=True,
        ),
        lax.all_to_all(
            margins.reshape(owners, cap), ("gx", "gy"), split_axis=0, concat_axis=0, tiled=True
        ),
        lax.all_to_all(
            labels.reshape(owners, cap), ("gx", "gy"), split_axis=0, concat_axis=0, tiled=True
        ),
    )
    got_center = got_center.reshape(owners * cap, 1024)
    got_error = got_error.reshape(owners * cap)
    got_label = got_label.reshape(owners * cap)
    bounds = jnp.stack([upper, lower])
    coeffs = jnp.concatenate([velocity, diffusivity[None]], axis=0)
    width = 1
    coeff_pad = with_halo(coeffs, (("gx", 2), ("gy", 3), ("gz", 1)), width)
    for step in range(2):
        padded = with_halo(bounds, (("gx", 2), ("gy", 3), ("gz", 1)), 1)
        bounds = advance(padded, coeff_pad)
    per_dev = depth // 16 * along_x * along_y
    target = jnp.where(got_label < 0.0, float(per_dev), got_label).astype(jnp.int32)
    high = got_center + got_error[:, None]
    low = got_center - got_error[:, None]
    ceiling = (
        jnp.full((per_dev, 1024), jnp.inf, dtype=jnp.float32).at[target].min(high, mode="drop")
    )
    floor_table = (
        jnp.full((per_dev, 1024), -jnp.inf, dtype=jnp.float32).at[target].max(low, mode="drop")
    )
    upper_out = from_blocks(jnp.minimum(to_blocks(bounds[0]), ceiling), depth, rows, cols)
    lower_out = from_blocks(jnp.maximum(to_blocks(bounds[1]), floor_table), depth, rows, cols)
    return (upper_out, lower_out)


def solution(mesh):
    in_specs = (
        P("gz", "gx", "gy"),
        P("gz", "gx", "gy"),
        P(None, "gz", "gx", "gy"),
        P("gz", "gx", "gy"),
        P("gz", ("gx", "gy"), None),
        P("gz", ("gx", "gy")),
        P("gz", ("gx", "gy")),
    )
    out_specs = (P("gz", "gx", "gy"), P("gz", "gx", "gy"))
    return jax.shard_map(shards, mesh=mesh, in_specs=in_specs, out_specs=out_specs, check_vma=False)
```

profile of v0, /device:TPU:26, one launch (start us, length us, event | category | flops | bytes accessed | tf_op | source)
XLA Modules:
  0.0 223.4 jit_solution(15293913470038820223)
XLA Ops:
  0.7 1.2 pad_maximum_fusion.59
  1.9 1.9 collective-permute-start
  3.8 3.6 %collective-permute-start.1 = (f32[4,16,1,128]{3,2,1,0:T(1,128)S(1)}, f32[4,16,1,128]{3,2,1,0:T(1,128)S(1)}, u32[]{:S(2)}, u32[]{:S(2)}) collective-permute-start(f32[4,16,1,128]{3,2,1,0:T(1,128)S(1)} %get-tuple-element.31), channel_id=1, source_target_pairs={{32,0},{64,32},{96,64},{128,96},{160,128},{192,160},{224,192},{256... | collective-permute-start | bytes 98312 | tf_op jit(solution)/shard_map/ppermute | solution.py:17
  7.5 3.1 %collective-permute-start.5 = (f32[2,16,1,128]{3,2,1,0:T(1,128)S(1)}, f32[2,16,1,128]{3,2,1,0:T(1,128)S(1)}, u32[]{:S(2)}, u32[]{:S(2)}) collective-permute-start(f32[2,16,1,128]{3,2,1,0:T(1,128)S(1)} %get-tuple-element.47), channel_id=1, source_target_pairs={{0,32},{32,64},{64,96},{96,128},{128,160},{160,192},{192,224},{224... | collective-permute-start | bytes 49160 | tf_op jit(solution)/shard_map/ppermute | solution.py:15
  10.6 2.5 %collective-permute-start.6 = (f32[2,16,1,128]{3,2,1,0:T(1,128)S(1)}, f32[2,16,1,128]{3,2,1,0:T(1,128)S(1)}, u32[]{:S(2)}, u32[]{:S(2)}) collective-permute-start(f32[2,16,1,128]{3,2,1,0:T(1,128)S(1)} %get-tuple-element.48), channel_id=1, source_target_pairs={{32,0},{64,32},{96,64},{128,96},{160,128},{192,160},{224,192},{256... | collective-permute-start | bytes 49160 | tf_op jit(solution)/shard_map/ppermute | solution.py:17
  13.6 2.5 %collective-permute-done.6 = f32[2,16,1,128]{3,2,1,0:T(1,128)S(1)} collective-permute-done((f32[2,16,1,128]{3,2,1,0:T(1,128)S(1)}, f32[2,16,1,128]{3,2,1,0:T(1,128)S(1)}, u32[]{:S(2)}, u32[]{:S(2)}) %collective-permute-start.6) | collective-permute-done | bytes 16416 | tf_op jit(solution)/shard_map/ppermute | solution.py:17
  16.2 10.9 %collective-permute-start.7 = (f32[2,16,10,1]{3,1,2,0:T(8,128)S(1)}, f32[2,16,10,1]{3,1,2,0:T(8,128)S(1)}, u32[]{:S(2)}, u32[]{:S(2)}) collective-permute-start(f32[2,16,10,1]{3,1,2,0:T(8,128)S(1)} %get-tuple-element.41), channel_id=1, source_target_pairs={{0,4},{4,8},{8,12},{12,16},{16,20},{20,24},{24,28},{1,5},{5,9},{9,... | collective-permute-start | bytes 3848 | tf_op jit(solution)/shard_map/ppermute | solution.py:15
  27.2 1.9 collective-permute-start.8
  29.1 1.0 scatter_custom_fusion
  30.1 0.8 all_to_all.15
  30.9 17.5 %all-to-all-start = ((f32[128,1,2]{2,1,0:T(1,128)}), f32[128,1,2]{2,1,0:T(1,128)S(1)}, u32[]{:S(2)}, u32[]{:S(2)}) async-start(f32[128,1,2]{2,1,0:T(1,128)} %bitcast.23), calls=%async_computation | async-start | bytes 131072 | tf_op jit(solution)/shard_map/all_to_all | solution.py:103
  48.4 1.1 scatter_custom_fusion.2
  49.5 0.8 all_to_all.18
  50.3 1.3 scatter_custom_fusion.1
  51.6 1.6 reshape.269
  53.2 0.2 pad_maximum_fusion.1
  53.4 3.4 %collective-permute-start.9 = (f32[2,1,10,130]{3,0,2,1:T(2,128)S(1)}, f32[2,1,10,130]{3,0,2,1:T(2,128)S(1)}, u32[]{:S(2)}, u32[]{:S(2)}) collective-permute-start(f32[2,1,10,130]{3,0,2,1:T(2,128)S(1)} %copy.207), channel_id=1, source_target_pairs={{0,1},{1,2},{2,3},{4,5},{5,6},{6,7},{8,9},{9,10},{10,11},{12,13},{... | collective-permute-start | bytes 31208 | tf_op jit(solution)/shard_map/ppermute | solution.py:15
  56.9 1.3 collective-permute-start.11
  58.3 0.2 fusion.56
  58.5 7.3 %collective-permute-start.3 = (f32[4,16,10,1]{3,2,1,0:T(8,128)S(1)}, f32[4,16,10,1]{3,2,1,0:T(8,128)S(1)}, u32[]{:S(2)}, u32[]{:S(2)}) collective-permute-start(f32[4,16,10,1]{3,2,1,0:T(8,128)S(1)} %get-tuple-element.22), channel_id=1, source_target_pairs={{4,0},{8,4},{12,8},{16,12},{20,16},{24,20},{28,24},{5,1},{9,5},{13... | collective-permute-start | bytes 7688 | tf_op jit(solution)/shard_map/ppermute | solution.py:17
  65.8 2.5 %collective-permute-start.2 = (f32[4,16,10,1]{3,2,1,0:T(8,128)S(1)}, f32[4,16,10,1]{3,2,1,0:T(8,128)S(1)}, u32[]{:S(2)}, u32[]{:S(2)}) collective-permute-start(f32[4,16,10,1]{3,2,1,0:T(8,128)S(1)} %get-tuple-element.21), channel_id=1, source_target_pairs={{0,4},{4,8},{8,12},{12,16},{16,20},{20,24},{24,28},{1,5},{5,9},{9,... | collective-permute-start | bytes 7688 | tf_op jit(solution)/shard_map/ppermute | solution.py:15
  68.3 0.9 pad_maximum_fusion.19
  69.2 1.0 copy.176
  70.2 0.6 copy.175
  70.8 0.6 copy.179
  71.4 7.9 %collective-permute-done.3 = f32[4,16,10,1]{3,2,1,0:T(8,128)S(1)} collective-permute-done((f32[4,16,10,1]{3,2,1,0:T(8,128)S(1)}, f32[4,16,10,1]{3,2,1,0:T(8,128)S(1)}, u32[]{:S(2)}, u32[]{:S(2)}) %collective-permute-start.3) | collective-permute-done | bytes 2592 | tf_op jit(solution)/shard_map/ppermute | solution.py:17
  79.3 21.3 %collective-permute-done.2 = f32[4,16,10,1]{3,2,1,0:T(8,128)S(1)} collective-permute-done((f32[4,16,10,1]{3,2,1,0:T(8,128)S(1)}, f32[4,16,10,1]{3,2,1,0:T(8,128)S(1)}, u32[]{:S(2)}, u32[]{:S(2)}) %collective-permute-start.2) | collective-permute-done | bytes 2592 | tf_op jit(solution)/shard_map/ppermute | solution.py:15
  100.8 1.3 collective-permute-start.10
  102.1 16.7 %collective-permute-start.4 = (f32[4,1,10,130]{3,2,1,0:T(8,128)S(1)}, f32[4,1,10,130]{3,2,1,0:T(8,128)}, u32[]{:S(2)}, u32[]{:S(2)}) collective-permute-start(f32[4,1,10,130]{3,2,1,0:T(8,128)S(1)} %get-tuple-element.18), channel_id=1, source_target_pairs={{0,1},{1,2},{2,3},{4,5},{5,6},{6,7},{8,9},{9,10},{10,11},{12,13},{... | collective-permute-start | bytes 62408 | tf_op jit(solution)/shard_map/ppermute | solution.py:15
  118.8 0.6 copy-done.22
  119.5 16.1 %all-to-all-start.2 = ((f32[128,1,2]{2,1,0:T(1,128)}), f32[128,1,2]{2,1,0:T(1,128)S(1)}, u32[]{:S(2)}, u32[]{:S(2)}) async-start(f32[128,1,2]{2,1,0:T(1,128)} %bitcast.27), calls=%async_computation.2 | async-start | bytes 131072 | tf_op jit(solution)/shard_map/all_to_all | solution.py:100
  135.7 10.7 %all-to-all-done.2 = f32[128,1,2]{2,1,0:T(1,128)S(1)} async-done(((f32[128,1,2]{2,1,0:T(1,128)}), f32[128,1,2]{2,1,0:T(1,128)S(1)}, u32[]{:S(2)}, u32[]{:S(2)}) %all-to-all-start.2) | async-done | bytes 1056 | tf_op jit(solution)/shard_map/all_to_all | solution.py:100
  146.4 0.6 copy-done.24
  147.1 9.2 %all-to-all-start.1 = ((f32[128,2,1024]{2,1,0:T(2,128)}), f32[128,2,1024]{2,1,0:T(2,128)S(1)}, u32[]{:S(2)}, u32[]{:S(2)}) async-start(f32[128,2,1024]{2,1,0:T(2,128)} %reshape.269), calls=%async_computation.1 | async-start | bytes 2097152 | tf_op jit(solution)/shard_map/all_to_all | solution.py:93
  156.4 0.9 fusion.41
  157.4 0.7 copy-done.21
  158.1 0.3 fusion.17
  158.4 2.1 collective-permute-start.12
  160.5 3.7 %collective-permute-start.13 = (f32[2,16,1,128]{3,2,1,0:T(1,128)S(1)}, f32[2,16,1,128]{3,2,1,0:T(1,128)S(1)}, u32[]{:S(2)}, u32[]{:S(2)}) collective-permute-start(f32[2,16,1,128]{3,2,1,0:T(1,128)S(1)} %get-tuple-element.46), channel_id=1, source_target_pairs={{32,0},{64,32},{96,64},{128,96},{160,128},{192,160},{224,192},{256... | collective-permute-start | bytes 49160 | tf_op jit(solution)/shard_map/ppermute | solution.py:17
  164.2 0.5 broadcast.428
  164.7 0.8 reduce.6
  165.7 13.9 %collective-permute-done.12 = f32[2,16,1,128]{3,2,1,0:T(1,128)S(1)} collective-permute-done((f32[2,16,1,128]{3,2,1,0:T(1,128)S(1)}, f32[2,16,1,128]{3,2,1,0:T(1,128)S(1)}, u32[]{:S(2)}, u32[]{:S(2)}) %collective-permute-start.12) | collective-permute-done | bytes 16416 | tf_op jit(solution)/shard_map/ppermute | solution.py:15
  179.7 7.3 %collective-permute-start.14 = (f32[2,16,10,1]{3,1,2,0:T(8,128)S(1)}, f32[2,16,10,1]{3,1,2,0:T(8,128)S(1)}, u32[]{:S(2)}, u32[]{:S(2)}) collective-permute-start(f32[2,16,10,1]{3,1,2,0:T(8,128)S(1)} %get-tuple-element.37), channel_id=1, source_target_pairs={{0,4},{4,8},{8,12},{12,16},{16,20},{20,24},{24,28},{1,5},{5,9},{9,... | collective-permute-start | bytes 3848 | tf_op jit(solution)/shard_map/ppermute | solution.py:15
  187.0 3.4 %collective-permute-start.15 = (f32[2,16,10,1]{3,1,2,0:T(8,128)S(1)}, f32[2,16,10,1]{3,1,2,0:T(8,128)S(1)}, u32[]{:S(2)}, u32[]{:S(2)}) collective-permute-start(f32[2,16,10,1]{3,1,2,0:T(8,128)S(1)} %get-tuple-element.38), channel_id=1, source_target_pairs={{4,0},{8,4},{12,8},{16,12},{20,16},{24,20},{28,24},{5,1},{9,5},{13... | collective-permute-start | bytes 3848 | tf_op jit(solution)/shard_map/ppermute | solution.py:17
  190.4 0.8 reduce.7
  191.3 0.7 collective-permute-done.14
  192.0 9.4 %collective-permute-done.15 = f32[2,16,10,1]{3,1,2,0:T(8,128)S(1)} collective-permute-done((f32[2,16,10,1]{3,1,2,0:T(8,128)S(1)}, f32[2,16,10,1]{3,1,2,0:T(8,128)S(1)}, u32[]{:S(2)}, u32[]{:S(2)}) %collective-permute-start.15) | collective-permute-done | bytes 1312 | tf_op jit(solution)/shard_map/ppermute | solution.py:17
  201.7 4.7 %collective-permute-start.16 = (f32[2,1,10,130]{3,0,2,1:T(2,128)S(1)}, f32[2,1,10,130]{3,0,2,1:T(2,128)S(1)}, u32[]{:S(2)}, u32[]{:S(2)}) collective-permute-start(f32[2,1,10,130]{3,0,2,1:T(2,128)S(1)} %copy.211), channel_id=1, source_target_pairs={{0,1},{1,2},{2,3},{4,5},{5,6},{6,7},{8,9},{9,10},{10,11},{12,13},{... | collective-permute-start | bytes 31208 | tf_op jit(solution)/shard_map/ppermute | solution.py:15
  206.4 1.3 collective-permute-start.17
  207.9 0.2 copy.187
  208.2 3.9 %collective-permute-done.17 = f32[2,1,10,130]{3,0,2,1:T(2,128)S(1)} collective-permute-done((f32[2,1,10,130]{3,0,2,1:T(2,128)S(1)}, f32[2,1,10,130]{3,0,2,1:T(2,128)S(1)}, u32[]{:S(2)}, u32[]{:S(2)}) %collective-permute-start.17) | collective-permute-done | bytes 10432 | tf_op jit(solution)/shard_map/ppermute | solution.py:17
  212.1 0.3 fusion.26
  212.4 0.2 copy.200
  212.6 0.5 copy.201
  213.3 0.2 copy.193
  213.6 0.5 copy.194
  214.3 0.7 reshape.270
  215.0 2.8 %scatter_custom_fusion.4 = f32[16,1024]{1,0:T(8,128)S(1)} fusion(s32[256]{0:T(256)S(1)} %bitcast.103, f32[256,1024]{1,0:T(8,128)S(1)} %reshape.270, f32[256]{0:T(256)S(1)} %add.239, f32[]{:T(128)} %constant.119.clone.1), kind=kCustom, calls=%fused_computation.5 | custom fusion | flops 524288 | bytes 1115140 | tf_op jit(solution)/shard_map/scatter-max | solution.py:125
  217.8 0.2 copy.203
  218.0 0.4 copy.204
  218.4 0.8 copy.206
  219.2 2.8 %scatter_custom_fusion.3 = f32[16,1024]{1,0:T(8,128)S(1)} fusion(s32[256]{0:T(256)S(1)} %bitcast.104, f32[256,1024]{1,0:T(8,128)S(1)} %reshape.270, f32[256]{0:T(256)S(1)} %add.239, f32[]{:T(128)} %constant.101.clone.1), kind=kCustom, calls=%fused_computation.7 | custom fusion | flops 524288 | bytes 1115140 | tf_op jit(solution)/shard_map/scatter-min | solution.py:122
  222.2 0.4 copy.199
  222.5 0.8 copy.205
  (105 shorter events, 2.7 us)
Async XLA Ops:
  0.6 49.6 %copy-start = (f32[1,128,1024]{2,1,0:T(8,128)S(1)}, f32[1,128,1024]{2,1,0:T(8,128)}, u32[]{:S(2)}) copy-start(f32[1,128,1024]{2,1,0:T(8,128)} %param.11) | copy-start | bytes 1572868
  0.6 6.8 %copy-start.10 = (f32[16,8,128]{2,1,0:T(8,128)S(1)}, f32[16,8,128]{2,1,0:T(8,128)}, u32[]{:S(2)}) copy-start(f32[16,8,128]{2,1,0:T(8,128)} %param.7) | copy-start | bytes 196612
  0.7 6.8 %copy-start.12 = (f32[16,8,128]{2,1,0:T(8,128)S(1)}, f32[16,8,128]{2,1,0:T(8,128)}, u32[]{:S(2)}) copy-start(f32[16,8,128]{2,1,0:T(8,128)} %param.8) | copy-start | bytes 196612
  1.9 56.3 %collective-permute-start = (f32[4,16,1,128]{3,2,1,0:T(1,128)S(1)}, f32[4,16,1,128]{3,2,1,0:T(1,128)S(1)}, u32[]{:S(2)}, u32[]{:S(2)}) collective-permute-start(f32[4,16,1,128]{3,2,1,0:T(1,128)S(1)} %get-tuple-element.30), channel_id=1, source_target_pairs={{0,32},{32,64},{64,96},{96,128},{128,160},{160,192},{192,224},{224... | collective-permute-start | bytes 98312 | tf_op jit(solution)/shard_map/ppermute | solution.py:15
  3.8 54.4 %collective-permute-start.1 = (f32[4,16,1,128]{3,2,1,0:T(1,128)S(1)}, f32[4,16,1,128]{3,2,1,0:T(1,128)S(1)}, u32[]{:S(2)}, u32[]{:S(2)}) collective-permute-start(f32[4,16,1,128]{3,2,1,0:T(1,128)S(1)} %get-tuple-element.31), channel_id=1, source_target_pairs={{32,0},{64,32},{96,64},{128,96},{160,128},{192,160},{224,192},{256... | collective-permute-start | bytes 98312 | tf_op jit(solution)/shard_map/ppermute | solution.py:17
  7.5 5.6 %copy-start.28 = (s32[1,128]{1,0:T(1,128)S(1)}, s32[1,128]{1,0:T(1,128)}, u32[]{:S(2)}) copy-start(s32[1,128]{1,0:T(1,128)} %param.13) | copy-start | bytes 1540
  7.5 6.1 %collective-permute-start.5 = (f32[2,16,1,128]{3,2,1,0:T(1,128)S(1)}, f32[2,16,1,128]{3,2,1,0:T(1,128)S(1)}, u32[]{:S(2)}, u32[]{:S(2)}) collective-permute-start(f32[2,16,1,128]{3,2,1,0:T(1,128)S(1)} %get-tuple-element.47), channel_id=1, source_target_pairs={{0,32},{32,64},{64,96},{96,128},{128,160},{160,192},{192,224},{224... | collective-permute-start | bytes 49160 | tf_op jit(solution)/shard_map/ppermute | solution.py:15
  10.6 5.5 %collective-permute-start.6 = (f32[2,16,1,128]{3,2,1,0:T(1,128)S(1)}, f32[2,16,1,128]{3,2,1,0:T(1,128)S(1)}, u32[]{:S(2)}, u32[]{:S(2)}) collective-permute-start(f32[2,16,1,128]{3,2,1,0:T(1,128)S(1)} %get-tuple-element.48), channel_id=1, source_target_pairs={{32,0},{64,32},{96,64},{128,96},{160,128},{192,160},{224,192},{256... | collective-permute-start | bytes 49160 | tf_op jit(solution)/shard_map/ppermute | solution.py:17
  16.1 52.2 %copy-start.20 = (f32[2,16,1,128]{3,2,1,0:T(1,128)}, f32[2,16,1,128]{3,2,1,0:T(1,128)S(1)}, u32[]{:S(2)}) copy-start(f32[2,16,1,128]{3,2,1,0:T(1,128)S(1)} %collective-permute-done.6) | copy-start | bytes 49156
  16.2 36.9 %collective-permute-start.7 = (f32[2,16,10,1]{3,1,2,0:T(8,128)S(1)}, f32[2,16,10,1]{3,1,2,0:T(8,128)S(1)}, u32[]{:S(2)}, u32[]{:S(2)}) collective-permute-start(f32[2,16,10,1]{3,1,2,0:T(8,128)S(1)} %get-tuple-element.41), channel_id=1, source_target_pairs={{0,4},{4,8},{8,12},{12,16},{16,20},{20,24},{24,28},{1,5},{5,9},{9,... | collective-permute-start | bytes 3848 | tf_op jit(solution)/shard_map/ppermute | solution.py:15
  27.2 26.0 %collective-permute-start.8 = (f32[2,16,10,1]{3,1,2,0:T(8,128)S(1)}, f32[2,16,10,1]{3,1,2,0:T(8,128)S(1)}, u32[]{:S(2)}, u32[]{:S(2)}) collective-permute-start(f32[2,16,10,1]{3,1,2,0:T(8,128)S(1)} %get-tuple-element.42), channel_id=1, source_target_pairs={{4,0},{8,4},{12,8},{16,12},{20,16},{24,20},{28,24},{5,1},{9,5},{13... | collective-permute-start | bytes 3848 | tf_op jit(solution)/shard_map/ppermute | solution.py:17
  30.9 87.9 %all-to-all-start = ((f32[128,1,2]{2,1,0:T(1,128)}), f32[128,1,2]{2,1,0:T(1,128)S(1)}, u32[]{:S(2)}, u32[]{:S(2)}) async-start(f32[128,1,2]{2,1,0:T(1,128)} %bitcast.23), calls=%async_computation | async-start | bytes 131072 | tf_op jit(solution)/shard_map/all_to_all | solution.py:103
  53.2 5.0 %copy-start.1 = (f32[3,16,8,128]{3,2,1,0:T(8,128)S(1)}, f32[3,16,8,128]{3,2,1,0:T(8,128)}, u32[]{:S(2)}) copy-start(f32[3,16,8,128]{3,2,1,0:T(8,128)} %param.9) | copy-start | bytes 589828
  53.4 4.8 %copy-start.2 = (f32[16,8,128]{2,1,0:T(8,128)S(1)}, f32[16,8,128]{2,1,0:T(8,128)}, u32[]{:S(2)}) copy-start(f32[16,8,128]{2,1,0:T(8,128)} %param.10) | copy-start | bytes 196612
  53.4 16.7 %collective-permute-start.9 = (f32[2,1,10,130]{3,0,2,1:T(2,128)S(1)}, f32[2,1,10,130]{3,0,2,1:T(2,128)S(1)}, u32[]{:S(2)}, u32[]{:S(2)}) collective-permute-start(f32[2,1,10,130]{3,0,2,1:T(2,128)S(1)} %copy.207), channel_id=1, source_target_pairs={{0,1},{1,2},{2,3},{4,5},{5,6},{6,7},{8,9},{9,10},{10,11},{12,13},{... | collective-permute-start | bytes 31208 | tf_op jit(solution)/shard_map/ppermute | solution.py:15
  56.9 13.9 %collective-permute-start.11 = (f32[2,1,10,130]{3,0,2,1:T(2,128)S(1)}, f32[2,1,10,130]{3,0,2,1:T(2,128)S(1)}, u32[]{:S(2)}, u32[]{:S(2)}) collective-permute-start(f32[2,1,10,130]{3,0,2,1:T(2,128)S(1)} %copy.208), channel_id=1, source_target_pairs={{1,0},{2,1},{3,2},{5,4},{6,5},{7,6},{9,8},{10,9},{11,10},{13,12},{... | collective-permute-start | bytes 31208 | tf_op jit(solution)/shard_map/ppermute | solution.py:17
  58.2 77.4 %copy-start.16 = (f32[4,16,1,128]{3,2,1,0:T(1,128)}, f32[4,16,1,128]{3,2,1,0:T(1,128)S(1)}, u32[]{:S(2)}) copy-start(f32[4,16,1,128]{3,2,1,0:T(1,128)S(1)} %collective-permute-done) | copy-start | bytes 98308
  58.2 77.3 %copy-start.18 = (f32[4,16,1,128]{3,2,1,0:T(1,128)}, f32[4,16,1,128]{3,2,1,0:T(1,128)S(1)}, u32[]{:S(2)}) copy-start(f32[4,16,1,128]{3,2,1,0:T(1,128)S(1)} %collective-permute-done.1) | copy-start | bytes 98308
  58.5 20.8 %collective-permute-start.3 = (f32[4,16,10,1]{3,2,1,0:T(8,128)S(1)}, f32[4,16,10,1]{3,2,1,0:T(8,128)S(1)}, u32[]{:S(2)}, u32[]{:S(2)}) collective-permute-start(f32[4,16,10,1]{3,2,1,0:T(8,128)S(1)} %get-tuple-element.22), channel_id=1, source_target_pairs={{4,0},{8,4},{12,8},{16,12},{20,16},{24,20},{28,24},{5,1},{9,5},{13... | collective-permute-start | bytes 7688 | tf_op jit(solution)/shard_map/ppermute | solution.py:17
  65.8 34.8 %collective-permute-start.2 = (f32[4,16,10,1]{3,2,1,0:T(8,128)S(1)}, f32[4,16,10,1]{3,2,1,0:T(8,128)S(1)}, u32[]{:S(2)}, u32[]{:S(2)}) collective-permute-start(f32[4,16,10,1]{3,2,1,0:T(8,128)S(1)} %get-tuple-element.21), channel_id=1, source_target_pairs={{0,4},{4,8},{8,12},{12,16},{16,20},{20,24},{24,28},{1,5},{5,9},{9,... | collective-permute-start | bytes 7688 | tf_op jit(solution)/shard_map/ppermute | solution.py:15
  100.8 55.5 %collective-permute-start.10 = (f32[4,1,10,130]{3,2,1,0:T(8,128)S(1)}, f32[4,1,10,130]{3,2,1,0:T(8,128)S(1)}, u32[]{:S(2)}, u32[]{:S(2)}) collective-permute-start(f32[4,1,10,130]{3,2,1,0:T(8,128)S(1)} %get-tuple-element.19), channel_id=1, source_target_pairs={{1,0},{2,1},{3,2},{5,4},{6,5},{7,6},{9,8},{10,9},{11,10},{13,12},{... | collective-permute-start | bytes 62408 | tf_op jit(solution)/shard_map/ppermute | solution.py:17
  102.1 54.2 %collective-permute-start.4 = (f32[4,1,10,130]{3,2,1,0:T(8,128)S(1)}, f32[4,1,10,130]{3,2,1,0:T(8,128)}, u32[]{:S(2)}, u32[]{:S(2)}) collective-permute-start(f32[4,1,10,130]{3,2,1,0:T(8,128)S(1)} %get-tuple-element.18), channel_id=1, source_target_pairs={{0,1},{1,2},{2,3},{4,5},{5,6},{6,7},{8,9},{9,10},{10,11},{12,13},{... | collective-permute-start | bytes 62408 | tf_op jit(solution)/shard_map/ppermute | solution.py:15
  118.8 0.6 copy-start.22
  119.5 27.0 %all-to-all-start.2 = ((f32[128,1,2]{2,1,0:T(1,128)}), f32[128,1,2]{2,1,0:T(1,128)S(1)}, u32[]{:S(2)}, u32[]{:S(2)}) async-start(f32[128,1,2]{2,1,0:T(1,128)} %bitcast.27), calls=%async_computation.2 | async-start | bytes 131072 | tf_op jit(solution)/shard_map/all_to_all | solution.py:100
  135.7 20.6 %copy-start.17 = (f32[4,16,1,128]{3,2,1,0:T(1,128)S(1)}, f32[4,16,1,128]{3,2,1,0:T(1,128)}, u32[]{:S(2)}) copy-start(f32[4,16,1,128]{3,2,1,0:T(1,128)} %copy-done.16) | copy-start | bytes 98308
  135.7 20.6 %copy-start.19 = (f32[4,16,1,128]{3,2,1,0:T(1,128)S(1)}, f32[4,16,1,128]{3,2,1,0:T(1,128)}, u32[]{:S(2)}) copy-start(f32[4,16,1,128]{3,2,1,0:T(1,128)} %copy-done.18) | copy-start | bytes 98308
  146.4 0.6 copy-start.24
  147.1 67.2 %all-to-all-start.1 = ((f32[128,2,1024]{2,1,0:T(2,128)}), f32[128,2,1024]{2,1,0:T(2,128)S(1)}, u32[]{:S(2)}, u32[]{:S(2)}) async-start(f32[128,2,1024]{2,1,0:T(2,128)} %reshape.269), calls=%async_computation.1 | async-start | bytes 2097152 | tf_op jit(solution)/shard_map/all_to_all | solution.py:93
  156.2 1.1 copy-start.3
  156.3 1.1 copy-start.14
  156.3 1.1 copy-start.15
  156.3 1.0 copy-start.11
  156.3 1.0 copy-start.13
  156.3 1.0 copy-start.26
  156.3 1.0 copy-start.27
  157.3 1.1 copy-start.4
  157.3 1.1 copy-start.6
  157.3 1.1 copy-start.8
  157.3 0.8 copy-start.21
  158.4 6.3 %copy-start.23 = (f32[128,1,2]{2,1,0:T(1,128)S(1)}, f32[128,1,2]{2,1,0:T(1,128)}, u32[]{:S(2)}) copy-start(f32[128,1,2]{2,1,0:T(1,128)} %copy-done.22) | copy-start | bytes 3076
  158.4 21.2 %collective-permute-start.12 = (f32[2,16,1,128]{3,2,1,0:T(1,128)S(1)}, f32[2,16,1,128]{3,2,1,0:T(1,128)S(1)}, u32[]{:S(2)}, u32[]{:S(2)}) collective-permute-start(f32[2,16,1,128]{3,2,1,0:T(1,128)S(1)} %get-tuple-element.45), channel_id=1, source_target_pairs={{0,32},{32,64},{64,96},{96,128},{128,160},{160,192},{192,224},{224... | collective-permute-start | bytes 49160 | tf_op jit(solution)/shard_map/ppermute | solution.py:15
  160.5 19.1 %collective-permute-start.13 = (f32[2,16,1,128]{3,2,1,0:T(1,128)S(1)}, f32[2,16,1,128]{3,2,1,0:T(1,128)S(1)}, u32[]{:S(2)}, u32[]{:S(2)}) collective-permute-start(f32[2,16,1,128]{3,2,1,0:T(1,128)S(1)} %get-tuple-element.46), channel_id=1, source_target_pairs={{32,0},{64,32},{96,64},{128,96},{160,128},{192,160},{224,192},{256... | collective-permute-start | bytes 49160 | tf_op jit(solution)/shard_map/ppermute | solution.py:17
  179.6 10.8 %copy-start.25 = (f32[128,1,2]{2,1,0:T(1,128)S(1)}, f32[128,1,2]{2,1,0:T(1,128)}, u32[]{:S(2)}) copy-start(f32[128,1,2]{2,1,0:T(1,128)} %copy-done.24) | copy-start | bytes 3076
  179.7 12.3 %collective-permute-start.14 = (f32[2,16,10,1]{3,1,2,0:T(8,128)S(1)}, f32[2,16,10,1]{3,1,2,0:T(8,128)S(1)}, u32[]{:S(2)}, u32[]{:S(2)}) collective-permute-start(f32[2,16,10,1]{3,1,2,0:T(8,128)S(1)} %get-tuple-element.37), channel_id=1, source_target_pairs={{0,4},{4,8},{8,12},{12,16},{16,20},{20,24},{24,28},{1,5},{5,9},{9,... | collective-permute-start | bytes 3848 | tf_op jit(solution)/shard_map/ppermute | solution.py:15
  187.0 14.4 %collective-permute-start.15 = (f32[2,16,10,1]{3,1,2,0:T(8,128)S(1)}, f32[2,16,10,1]{3,1,2,0:T(8,128)S(1)}, u32[]{:S(2)}, u32[]{:S(2)}) collective-permute-start(f32[2,16,10,1]{3,1,2,0:T(8,128)S(1)} %get-tuple-element.38), channel_id=1, source_target_pairs={{4,0},{8,4},{12,8},{16,12},{20,16},{24,20},{28,24},{5,1},{9,5},{13... | collective-permute-start | bytes 3848 | tf_op jit(solution)/shard_map/ppermute | solution.py:17
  201.7 6.5 %collective-permute-start.16 = (f32[2,1,10,130]{3,0,2,1:T(2,128)S(1)}, f32[2,1,10,130]{3,0,2,1:T(2,128)S(1)}, u32[]{:S(2)}, u32[]{:S(2)}) collective-permute-start(f32[2,1,10,130]{3,0,2,1:T(2,128)S(1)} %copy.211), channel_id=1, source_target_pairs={{0,1},{1,2},{2,3},{4,5},{5,6},{6,7},{8,9},{9,10},{10,11},{12,13},{... | collective-permute-start | bytes 31208 | tf_op jit(solution)/shard_map/ppermute | solution.py:15
  206.4 5.7 %collective-permute-start.17 = (f32[2,1,10,130]{3,0,2,1:T(2,128)S(1)}, f32[2,1,10,130]{3,0,2,1:T(2,128)S(1)}, u32[]{:S(2)}, u32[]{:S(2)}) collective-permute-start(f32[2,1,10,130]{3,0,2,1:T(2,128)S(1)} %copy.212), channel_id=1, source_target_pairs={{1,0},{2,1},{3,2},{5,4},{6,5},{7,6},{9,8},{10,9},{11,10},{13,12},{... | collective-permute-start | bytes 31208 | tf_op jit(solution)/shard_map/ppermute | solution.py:17
  207.9 4.2 %copy-start.7 = (f32[16,8,128]{2,1,0:T(8,128)S(1)}, f32[16,8,128]{2,1,0:T(8,128)}, u32[]{:S(2)}) copy-start(f32[16,8,128]{2,1,0:T(8,128)} %copy-done.6) | copy-start | bytes 196612
  207.9 4.2 %copy-start.9 = (f32[16,8,128]{2,1,0:T(8,128)S(1)}, f32[16,8,128]{2,1,0:T(8,128)}, u32[]{:S(2)}) copy-start(f32[16,8,128]{2,1,0:T(8,128)} %copy-done.8) | copy-start | bytes 196612
  208.1 4.0 %copy-start.5 = (f32[16,8,128]{2,1,0:T(8,128)S(1)}, f32[16,8,128]{2,1,0:T(8,128)}, u32[]{:S(2)}) copy-start(f32[16,8,128]{2,1,0:T(8,128)} %copy-done.4) | copy-start | bytes 196612
where the time goes:
time: 224 us; the launch traced here: 223 us
  starting transfers between devices  122 us (54%)
  waiting for transfers between devices  70.4 us (31%)
  local copies, waits for them, and re-layouts  17.8 us (8%)
  other arithmetic  12.1 us (5%)
    ppermute x9, starting transfers between devices, with_halo(): lax.ppermute(tail, axis, [(i, (i + 1) % count) for i in range(ends)])  52.6 us
    ppermute x9, waiting for transfers between devices, with_halo(): lax.ppermute(tail, axis, [(i, (i + 1) % count) for i in range(ends)])  35.9 us
    ppermute x9, starting transfers between devices, with_halo(): lax.ppermute(head, axis, [((i + 1) % count, i) for i in range(ends)])  26.2 us
    ppermute x9, waiting for transfers between devices, with_halo(): lax.ppermute(head, axis, [((i + 1) % count, i) for i in range(ends)])  23.8 us
    all_to_all x1, starting transfers between devices, shards(): lax.all_to_all(labels.reshape(owners, cap), ('gx', 'gy'), split_axis=0, c...  17.5 us
    all_to_all x1, starting transfers between devices, shards(): lax.all_to_all(margins.reshape(owners, cap), ('gx', 'gy'), split_axis=0,...  16.1 us
    all_to_all x1, waiting for transfers between devices, shards(): lax.all_to_all(margins.reshape(owners, cap), ('gx', 'gy'), split_axis=0,...  10.7 us
    all_to_all x1, starting transfers between devices, shards(): lax.all_to_all(outgoing.reshape(owners, cap, 1024), ('gx', 'gy'), split_a...  9.16 us
  transfers between devices with their start and end apart: 21, of which 8 were waited for; matrix products, arithmetic and copies ran while one was open for 7% of the time, Pallas kernels for 0%

commit v1 on v0

v1 whole, which is shorter than its diff:
```python
import jax
import jax.numpy as jnp
from jax import lax
from jax.experimental import pallas as pl
from jax.experimental.pallas import tpu as pltpu
from jax.sharding import PartitionSpec as P

MESH = pl.DeviceIdType.MESH
N_X, N_Y, N_Z = 16, 8, 4
OWNERS = N_X * N_Y
GROUP = 16
GROUPS = OWNERS // GROUP
ROWS = 17
PITCH = 24
UP, LO, VZ, VX, VY, DIFF = range(6)


def peer(i, gx, gy):
    along_y = lax.rem(gx // 2 + lax.rem(i, 8), 8)
    core = lax.rem(lax.rem(gx, 2) + lax.rem(i // 8, 2), 2)
    return along_y * 2 + core, lax.rem(gy + i // 16, N_Y)


def lane_of(shape):
    return lax.broadcasted_iota(jnp.int32, shape, len(shape) - 1)


def merge(tables, block, err, label):
    ceilings, floors = tables
    high = block + err
    low = block - err
    new_c, new_f = [], []
    for b in range(16):
        mine = label == float(b)
        new_c.append(jnp.minimum(ceilings[b], jnp.where(mine, high, jnp.inf)))
        new_f.append(jnp.maximum(floors[b], jnp.where(mine, low, -jnp.inf)))
    return tuple(new_c), tuple(new_f)


def regroup(table):
    rows = list(table)
    group = lane_of((8, 128)) // 8
    for k in (1, 2, 4, 8):
        high = lax.rem(group // k, 2) == 1
        for i in range(16):
            if i & k == 0:
                a, b = rows[i], rows[i | k]
                rows[i] = jnp.where(high, pltpu.roll(b, 8 * k, 1), a)
                rows[i | k] = jnp.where(high, b, pltpu.roll(a, 128 - 8 * k, 1))
    return rows


def kernel(
    upper, lower, velocity, diffusivity, center, error, block,
    upper_out, lower_out,
    fields, coefs, stage, err_v, blk_v, msg, got, ceil_t, floor_t, flat,
    zs, zr, xs, xr, ys, yr, turn,
    in_sem, c_sem, send_sem, recv_sem, face_send, face_recv,
):
    gx, gy, gz = lax.axis_index("gx"), lax.axis_index("gy"), lax.axis_index("gz")

    barrier = pltpu.get_barrier_semaphore()

    def greet(i, carry):
        px, py = peer(i, gx, gy)
        pl.semaphore_signal(barrier, inc=1, device_id=(px, py, gz), device_id_type=MESH)
        return carry

    lax.fori_loop(1, OWNERS, greet, 0)
    for d in (1, N_Z - 1):
        pl.semaphore_signal(
            barrier, inc=1, device_id=(gx, gy, lax.rem(gz + d, N_Z)), device_id_type=MESH
        )

    loads = [
        pltpu.make_async_copy(error, err_v, c_sem.at[0]),
        pltpu.make_async_copy(block, blk_v, c_sem.at[1]),
        pltpu.make_async_copy(center.at[0], stage, c_sem.at[2]),
    ]
    field_loads = [
        pltpu.make_async_copy(upper, fields.at[UP], in_sem.at[0]),
        pltpu.make_async_copy(lower, fields.at[LO], in_sem.at[1]),
        pltpu.make_async_copy(velocity, fields.at[pl.ds(VZ, 3)], in_sem.at[2]),
        pltpu.make_async_copy(diffusivity, fields.at[DIFF], in_sem.at[3]),
    ]
    for c in loads + field_loads:
        c.start()

    loads[0].wait()
    loads[1].wait()
    blk = blk_v[...]
    block_y = jnp.bitwise_and(blk, 127)
    owner = (blk // 128) * N_Y + block_y // 16
    local = jnp.bitwise_and(block_y, 15).astype(jnp.float32)
    dest = lax.broadcasted_iota(jnp.int32, (OWNERS, 128), 0)
    sensor = lane_of((OWNERS, 128))
    goes = jnp.broadcast_to(owner, (OWNERS, 128)) == dest
    before = jnp.where(dest < sensor, 1.0, 0.0).astype(jnp.bfloat16)
    rank = jnp.dot(
        jnp.where(goes, 1.0, 0.0).astype(jnp.bfloat16), before, preferred_element_type=jnp.float32
    )
    picks = [jnp.logical_and(goes, rank < 0.5), jnp.logical_and(goes, rank > 0.5)]
    meta = jnp.full((OWNERS, 128), -1.0, jnp.float32)
    for r in range(2):
        e = jnp.sum(jnp.where(picks[r], err_v[...], 0.0), axis=1, keepdims=True)
        l = jnp.sum(jnp.where(picks[r], local + 1.0, 0.0), axis=1, keepdims=True) - 1.0
        meta = jnp.where(sensor == 2 * r, e, meta)
        meta = jnp.where(sensor == 2 * r + 1, l, meta)
    msg[pl.ds(16, OWNERS, stride=PITCH), :] = meta
    pick = jnp.concatenate([jnp.where(p, 1.0, 0.0) for p in picks], axis=0).astype(jnp.bfloat16)
    loads[2].wait()
    for j in range(8):
        whole = stage[:, j * 128 : (j + 1) * 128]
        part_a = whole.astype(jnp.bfloat16)
        rest = whole - part_a.astype(jnp.float32)
        part_b = rest.astype(jnp.bfloat16)
        part_c = (rest - part_b.astype(jnp.float32)).astype(jnp.bfloat16)
        out = jnp.dot(pick, part_a, preferred_element_type=jnp.float32)
        out += jnp.dot(pick, part_b, preferred_element_type=jnp.float32)
        out += jnp.dot(pick, part_c, preferred_element_type=jnp.float32)
        msg[pl.ds(j, OWNERS, stride=PITCH), :] = out[:OWNERS]
        msg[pl.ds(8 + j, OWNERS, stride=PITCH), :] = out[OWNERS:]

    for c in field_loads:
        c.wait()

    def fill_faces(values, speeds):
        for k, v in enumerate(values):
            zs[0, 8 * k : 8 * k + 8, :] = v[15]
            zs[1, 8 * k : 8 * k + 8, :] = v[0]
            xs[0, 16 * k : 16 * k + 16, :] = v[:, 7, :]
            xs[1, 16 * k : 16 * k + 16, :] = v[:, 0, :]
            t = v.reshape(128, 128).T
            ys[0, k : k + 1, :] = t[127:128]
            ys[1, k : k + 1, :] = t[0:1]
        if speeds is not None:
            vz, vx, vy = speeds
            zs[0, 16:24, :] = vz[15]
            zs[1, 16:24, :] = vz[0]
            xs[0, 32:48, :] = vx[:, 7, :]
            xs[1, 32:48, :] = vx[:, 0, :]
            t = vy.reshape(128, 128).T
            ys[0, 2:3, :] = t[127:128]
            ys[1, 2:3, :] = t[0:1]

    def face_copies(rnd):
        copies = []
        for d in range(2):
            step = 1 if d == 0 else -1
            for k, (src, dst, dev) in enumerate((
                (zs, zr, (gx, gy, lax.rem(gz + step + N_Z, N_Z))),
                (xs, xr, (lax.rem(gx + step + N_X, N_X), gy, gz)),
                (ys, yr, (gx, lax.rem(gy + step + N_Y, N_Y), gz)),
            )):
                n = src.shape[1]
                if rnd == 1 and k < 2:
                    n = n // 3 * 2
                copies.append(
                    pltpu.make_async_remote_copy(
                        src_ref=src.at[d, pl.ds(0, n)],
                        dst_ref=dst.at[rnd, d, pl.ds(0, n)],
                        send_sem=face_send.at[rnd, d, k],
                        recv_sem=face_recv.at[rnd, d, k],
                        device_id=dev,
                        device_id_type=MESH,
                    )
                )
        return copies

    fill_faces([fields[UP], fields[LO]], [fields[VZ], fields[VX], fields[VY]])

    pl.semaphore_wait(barrier, OWNERS - 1 + 2)

    first = face_copies(0)
    for c in first:
        c.start()

    def message(i):
        px, py = peer(i, gx, gy)
        at = pl.multiple_of((px * N_Y + py) * PITCH, 8)
        return pltpu.make_async_remote_copy(
            src_ref=msg.at[pl.ds(at, ROWS)],
            dst_ref=got.at[i, pl.ds(0, ROWS)],
            send_sem=send_sem,
            recv_sem=recv_sem.at[i // GROUP],
            device_id=(px, py, gz),
            device_id_type=MESH,
        )

    def send(i, carry):
        message(i).start()
        return carry

    lax.fori_loop(1, OWNERS, send, 0)

    x_of = lax.broadcasted_iota(jnp.int32, (16, 8, 128), 1)
    y_of = lax.broadcasted_iota(jnp.int32, (16, 8, 128), 2)
    inner = [
        (gz > 0, gz < N_Z - 1),
        (gx > 0, gx < N_X - 1),
        (gy > 0, gy < N_Y - 1),
    ]

    def keep(flag, value):
        return jnp.where(flag, value, 0.0)

    def halo(rnd, dim, k, side):
        flag = inner[dim][side]
        if dim == 0:
            return keep(flag, zr[rnd, side, 8 * k : 8 * k + 8, :])[None]
        if dim == 1:
            return keep(flag, xr[rnd, side, 16 * k : 16 * k + 16, :])[:, None, :]
        columns = turned[side][:, k : k + 1]
        return keep(flag, columns).reshape(16, 8, 1)

    def shifted(value, rnd, dim, k):
        below, above = halo(rnd, dim, k, 0), halo(rnd, dim, k, 1)
        if dim == 0:
            return (
                jnp.concatenate([below, value[:15]], axis=0),
                jnp.concatenate([value[1:], above], axis=0),
            )
        if dim == 1:
            return (
                jnp.where(x_of == 0, below, pltpu.roll(value, 1, 1)),
                jnp.where(x_of == 7, above, pltpu.roll(value, 7, 1)),
            )
        return (
            jnp.where(y_of == 0, below, pltpu.roll(value, 1, 2)),
            jnp.where(y_of == 127, above, pltpu.roll(value, 127, 2)),
        )

    turn[...] = jnp.zeros_like(turn)

    def turn_faces(rnd):
        sides = []
        for d in range(2):
            turn[d, 0:8, :] = yr[rnd, d]
            sides.append(turn[d].T)
        return sides

    for c in first:
        c.wait()
    turned = turn_faces(0)
    diff = fields[DIFF]
    centre = 1.0 - 6.0 * diff
    for dim, which in enumerate((VZ, VX, VY)):
        v = fields[which]
        centre = centre - jnp.abs(v)
        v_below, v_above = shifted(v, 0, dim, 2)
        coefs[2 * dim] = jnp.maximum(v_below, 0.0) + diff
        coefs[2 * dim + 1] = jnp.maximum(-v_above, 0.0) + diff
    coefs[6] = centre

    def advance(rnd):
        results = []
        for k in range(2):
            value = fields[k]
            total = coefs[6] * value
            for dim in range(3):
                below, above = shifted(value, rnd, dim, k)
                total = total + coefs[2 * dim] * below + coefs[2 * dim + 1] * above
            results.append(total)
        return results

    once = advance(0)
    fields[UP] = once[0]
    fields[LO] = once[1]
    fill_faces([fields[UP], fields[LO]], None)
    second = face_copies(1)
    for c in second:
        c.start()

    def tables():
        return (
            tuple(ceil_t[b] for b in range(16)),
            tuple(floor_t[b] for b in range(16)),
        )

    def store(t):
        for b in range(16):
            ceil_t[b] = t[0][b]
            floor_t[b] = t[1][b]

    def take(t, rows, meta):
        for r in range(2):
            err = jnp.broadcast_to(meta[:, 2 * r : 2 * r + 1], (8, 128))
            label = jnp.broadcast_to(meta[:, 2 * r + 1 : 2 * r + 2], (8, 128))
            t = merge(t, rows(r), err, label)
        return t

    full = lambda v: jnp.full((8, 128), v, jnp.float32)
    own = (gx * N_Y + gy) * PITCH
    start = (tuple(full(jnp.inf) for _ in range(16)), tuple(full(-jnp.inf) for _ in range(16)))
    store(
        take(
            start,
            lambda r: msg[pl.ds(pl.multiple_of(own + 8 * r, 8), 8), :],
            msg[pl.ds(pl.multiple_of(own + 16, 8), 8), :][0:1],
        )
    )

    def await_group(g):
        lo = max(g * GROUP, 1)
        n = (g + 1) * GROUP - lo
        for_all = pltpu.make_async_remote_copy(
            src_ref=got.at[pl.ds(lo, n), pl.ds(0, ROWS)],
            dst_ref=got.at[pl.ds(lo, n), pl.ds(0, ROWS)],
            send_sem=send_sem,
            recv_sem=recv_sem.at[g],
            device_id=(gx, gy, gz),
            device_id_type=MESH,
        )
        for_all.wait_recv()

        def body(i, t):
            return take(t, lambda r: got[i, 8 * r : 8 * r + 8, :], got[i, 16:24, :][0:1])

        store(lax.fori_loop(lo, lo + n, body, tables()))

    await_group(0)

    for c in second:
        c.wait()
    turned = turn_faces(1)
    twice = advance(1)
    fields[UP] = twice[0]
    fields[LO] = twice[1]

    for g in range(1, GROUPS):
        await_group(g)

    for table, which, out in ((ceil_t, UP, upper_out), (floor_t, LO, lower_out)):
        rows = regroup([table[b] for b in range(16)])
        for g in range(16):
            flat[pl.ds(g, 8, stride=16), :] = rows[g]
        pick_of = jnp.minimum if which == UP else jnp.maximum
        out[...] = pick_of(fields[which], flat[...].reshape(16, 8, 128))

    def sent(i, carry):
        message(i).wait_send()
        return carry

    lax.fori_loop(1, OWNERS, sent, 0)


def shards(*args):
    f32 = jnp.float32
    dma = pltpu.SemaphoreType.DMA
    return pl.pallas_call(
        kernel,
        out_shape=[jax.ShapeDtypeStruct((16, 8, 128), f32)] * 2,
        in_specs=[pl.BlockSpec(memory_space=pl.ANY)] * 7,
        out_specs=[pl.BlockSpec(memory_space=pltpu.VMEM)] * 2,
        scratch_shapes=[
            pltpu.VMEM((6, 16, 8, 128), f32),
            pltpu.VMEM((7, 16, 8, 128), f32),
            pltpu.VMEM((128, 1024), f32),
            pltpu.VMEM((1, 128), f32),
            pltpu.VMEM((1, 128), jnp.int32),
            pltpu.VMEM((OWNERS * PITCH, 128), f32),
            pltpu.VMEM((OWNERS, PITCH, 128), f32),
            pltpu.VMEM((16, 8, 128), f32),
            pltpu.VMEM((16, 8, 128), f32),
            pltpu.VMEM((128, 128), f32),
            pltpu.VMEM((2, 24, 128), f32),
            pltpu.VMEM((2, 2, 24, 128), f32),
            pltpu.VMEM((2, 48, 128), f32),
            pltpu.VMEM((2, 2, 48, 128), f32),
            pltpu.VMEM((2, 8, 128), f32),
            pltpu.VMEM((2, 2, 8, 128), f32),
            pltpu.VMEM((2, 128, 128), f32),
            dma((4,)),
            dma((3,)),
            dma,
            dma((GROUPS,)),
            dma((2, 2, 3)),
            dma((2, 2, 3)),
        ],
        compiler_params=pltpu.CompilerParams(
            collective_id=0, has_side_effects=True, vmem_limit_bytes=32 << 20
        ),
        cost_estimate=pl.CostEstimate(flops=10**8, bytes_accessed=2 << 20, transcendentals=0),
    )(*args)


def solution(mesh):
    in_specs = (
        P("gz", "gx", "gy"),
        P("gz", "gx", "gy"),
        P(None, "gz", "gx", "gy"),
        P("gz", "gx", "gy"),
        P("gz", ("gx", "gy"), None),
        P("gz", ("gx", "gy")),
        P("gz", ("gx", "gy")),
    )
    out_specs = (P("gz", "gx", "gy"), P("gz", "gx", "gy"))
    return jax.shard_map(shards, mesh=mesh, in_specs=in_specs, out_specs=out_specs, check_vma=False)
```

time: 224 us -> 71.3 us (0.32)
  the two profiles are of different devices: /device:TPU:26 before, /device:TPU:1 now
where the time goes in v1:
time: 71.3 us; the launch traced here: 70.9 us
  Pallas kernels  63.2 us (89%)
  local copies, waits for them, and re-layouts  7.05 us (10%)
    pallas_call x1, Pallas kernels, shards(): pl.pallas_call(kernel, out_shape=[jax.ShapeDtypeStruct((16, 8, 128), f32)...  63.2 us
    unnamed x16, local copies, waits for them, and re-layouts  7.05 us

profile of v1, /device:TPU:1, one launch (start us, length us, event | category | flops | bytes accessed | tf_op | source)
XLA Modules:
  0.0 70.9 jit_solution(14425011481363995482)
XLA Ops:
  0.6 0.0 copy-start
  0.6 1.0 %copy-done = f32[1,128,1024]{2,1,0:T(8,128)S(1)} copy-done((f32[1,128,1024]{2,1,0:T(8,128)S(1)}, f32[1,128,1024]{2,1,0:T(8,128)}, u32[]{:S(2)}) %copy-start) | copy-done | bytes 524312
  1.7 0.0 copy-start.1
  1.7 0.9 %copy-done.1 = f32[3,16,8,128]{3,2,1,0:T(8,128)S(1)} copy-done((f32[3,16,8,128]{3,2,1,0:T(8,128)S(1)}, f32[3,16,8,128]{3,2,1,0:T(8,128)}, u32[]{:S(2)}) %copy-start.1) | copy-done | bytes 196632
  2.6 0.0 copy-start.2
  2.6 0.8 %copy-done.2 = f32[16,8,128]{2,1,0:T(8,128)S(1)} copy-done((f32[16,8,128]{2,1,0:T(8,128)S(1)}, f32[16,8,128]{2,1,0:T(8,128)}, u32[]{:S(2)}) %copy-start.2) | copy-done | bytes 65560
  3.4 0.0 copy-start.3
  3.4 0.8 %copy-done.3 = f32[16,8,128]{2,1,0:T(8,128)S(1)} copy-done((f32[16,8,128]{2,1,0:T(8,128)S(1)}, f32[16,8,128]{2,1,0:T(8,128)}, u32[]{:S(2)}) %copy-start.3) | copy-done | bytes 65560
  4.3 0.0 copy-start.4
  4.3 0.8 %copy-done.4 = f32[16,8,128]{2,1,0:T(8,128)S(1)} copy-done((f32[16,8,128]{2,1,0:T(8,128)S(1)}, f32[16,8,128]{2,1,0:T(8,128)}, u32[]{:S(2)}) %copy-start.4) | copy-done | bytes 65560
  5.1 0.0 copy-start.5
  5.1 0.7 copy-done.5
  5.8 0.0 copy-start.6
  5.8 0.7 copy-done.6
  6.4 63.2 %shard_map.86 = (f32[16,8,128]{2,1,0:T(8,128)S(1)}, f32[16,8,128]{2,1,0:T(8,128)S(1)}) custom-call(f32[16,8,128]{2,1,0:T(8,128)S(1)} %copy-done.2, f32[16,8,128]{2,1,0:T(8,128)S(1)} %copy-done.3, f32[3,16,8,128]{3,2,1,0:T(8,128)S(1)} %copy-done.1, f32[16,8,128]{2,1,0:T(8,128)S(1)} %copy-done.4, f32[1,128,1024]{2,1,0:T(8,128)S(1)} %copy-done, ...), custom_call_target="tpu_custom_call" | custom-call | flops 100000000 | bytes 2097152 | tf_op jit(solution)/shard_map/pallas_call | solution.py:350
  69.6 0.6 copy.11
  70.2 0.6 copy.12
Async XLA Ops:
  0.6 1.0 %copy-start = (f32[1,128,1024]{2,1,0:T(8,128)S(1)}, f32[1,128,1024]{2,1,0:T(8,128)}, u32[]{:S(2)}) copy-start(f32[1,128,1024]{2,1,0:T(8,128)} %center.1) | copy-start | bytes 1572868
  1.7 0.9 %copy-start.1 = (f32[3,16,8,128]{3,2,1,0:T(8,128)S(1)}, f32[3,16,8,128]{3,2,1,0:T(8,128)}, u32[]{:S(2)}) copy-start(f32[3,16,8,128]{3,2,1,0:T(8,128)} %velocity.1) | copy-start | bytes 589828
  2.6 0.8 %copy-start.2 = (f32[16,8,128]{2,1,0:T(8,128)S(1)}, f32[16,8,128]{2,1,0:T(8,128)}, u32[]{:S(2)}) copy-start(f32[16,8,128]{2,1,0:T(8,128)} %upper.1) | copy-start | bytes 196612
  3.4 0.8 %copy-start.3 = (f32[16,8,128]{2,1,0:T(8,128)S(1)}, f32[16,8,128]{2,1,0:T(8,128)}, u32[]{:S(2)}) copy-start(f32[16,8,128]{2,1,0:T(8,128)} %lower.1) | copy-start | bytes 196612
  4.3 0.8 %copy-start.4 = (f32[16,8,128]{2,1,0:T(8,128)S(1)}, f32[16,8,128]{2,1,0:T(8,128)}, u32[]{:S(2)}) copy-start(f32[16,8,128]{2,1,0:T(8,128)} %diffusivity.1) | copy-start | bytes 196612
  5.1 0.7 copy-start.5
  5.8 0.7 copy-start.6

commit v2 on v1

--- a/solution.py
+++ b/solution.py
@@ -16,9 +16,9 @@
 
 
 def peer(i, gx, gy):
-    along_y = lax.rem(gx // 2 + lax.rem(i, 8), 8)
-    core = lax.rem(lax.rem(gx, 2) + lax.rem(i // 8, 2), 2)
-    return along_y * 2 + core, lax.rem(gy + i // 16, N_Y)
+    along_x = ((gx >> 1) + i) & 7
+    core = (gx ^ (i >> 3)) & 1
+    return along_x * 2 + core, (gy + (i >> 4)) & (N_Y - 1)
 
 
 def lane_of(shape):
@@ -54,23 +54,10 @@
     upper, lower, velocity, diffusivity, center, error, block,
     upper_out, lower_out,
     fields, coefs, stage, err_v, blk_v, msg, got, ceil_t, floor_t, flat,
-    zs, zr, xs, xr, ys, yr, turn,
+    zs, zr, xs, xr, ys, yr, turn, wide,
     in_sem, c_sem, send_sem, recv_sem, face_send, face_recv,
 ):
     gx, gy, gz = lax.axis_index("gx"), lax.axis_index("gy"), lax.axis_index("gz")
-
-    barrier = pltpu.get_barrier_semaphore()
-
-    def greet(i, carry):
-        px, py = peer(i, gx, gy)
-        pl.semaphore_signal(barrier, inc=1, device_id=(px, py, gz), device_id_type=MESH)
-        return carry
-
-    lax.fori_loop(1, OWNERS, greet, 0)
-    for d in (1, N_Z - 1):
-        pl.semaphore_signal(
-            barrier, inc=1, device_id=(gx, gy, lax.rem(gz + d, N_Z)), device_id_type=MESH
-        )
 
     loads = [
         pltpu.make_async_copy(error, err_v, c_sem.at[0]),
@@ -85,6 +72,19 @@
     ]
     for c in loads + field_loads:
         c.start()
+
+    barrier = pltpu.get_barrier_semaphore()
+
+    def greet(i, carry):
+        px, py = peer(i, gx, gy)
+        pl.semaphore_signal(barrier, inc=1, device_id=(px, py, gz), device_id_type=MESH)
+        return carry
+
+    lax.fori_loop(1, OWNERS, greet, 0)
+    for d in (1, N_Z - 1):
+        pl.semaphore_signal(
+            barrier, inc=1, device_id=(gx, gy, lax.rem(gz + d, N_Z)), device_id_type=MESH
+        )
 
     loads[0].wait()
     loads[1].wait()
@@ -182,7 +182,7 @@
             src_ref=msg.at[pl.ds(at, ROWS)],
             dst_ref=got.at[i, pl.ds(0, ROWS)],
             send_sem=send_sem,
-            recv_sem=recv_sem.at[i // GROUP],
+            recv_sem=recv_sem.at[i >> 4],
             device_id=(px, py, gz),
             device_id_type=MESH,
         )
@@ -282,23 +282,20 @@
             ceil_t[b] = t[0][b]
             floor_t[b] = t[1][b]
 
-    def take(t, rows, meta):
+    def spread(m, row):
+        for k in range(4):
+            wide[4 * m + k] = jnp.broadcast_to(row[:, k : k + 1], (8, 128))
+
+    def take(t, m, rows):
         for r in range(2):
-            err = jnp.broadcast_to(meta[:, 2 * r : 2 * r + 1], (8, 128))
-            label = jnp.broadcast_to(meta[:, 2 * r + 1 : 2 * r + 2], (8, 128))
-            t = merge(t, rows(r), err, label)
+            t = merge(t, rows(r), wide[4 * m + 2 * r], wide[4 * m + 2 * r + 1])
         return t
 
     full = lambda v: jnp.full((8, 128), v, jnp.float32)
     own = (gx * N_Y + gy) * PITCH
     start = (tuple(full(jnp.inf) for _ in range(16)), tuple(full(-jnp.inf) for _ in range(16)))
-    store(
-        take(
-            start,
-            lambda r: msg[pl.ds(pl.multiple_of(own + 8 * r, 8), 8), :],
-            msg[pl.ds(pl.multiple_of(own + 16, 8), 8), :][0:1],
-        )
-    )
+    spread(0, msg[pl.ds(pl.multiple_of(own + 16, 8), 8), :][0:1])
+    store(take(start, 0, lambda r: msg[pl.ds(pl.multiple_of(own + 8 * r, 8), 8), :]))
 
     def await_group(g):
         lo = max(g * GROUP, 1)
@@ -312,11 +309,17 @@
             device_id_type=MESH,
         )
         for_all.wait_recv()
-
-        def body(i, t):
-            return take(t, lambda r: got[i, 8 * r : 8 * r + 8, :], got[i, 16:24, :][0:1])
-
-        store(lax.fori_loop(lo, lo + n, body, tables()))
+        for m in range(n):
+            spread(m, got[lo + m, 16:17, :])
+
+        def one(m, t):
+            return take(t, m, lambda r: got[lo + m, 8 * r : 8 * r + 8, :])
+
+        def body(h, t):
+            return one(2 * h + 1, one(2 * h, t))
+
+        t = lax.fori_loop(0, n // 2, body, tables())
+        store(one(n - 1, t) if n % 2 else t)
 
     await_group(0)
 
@@ -370,6 +373,7 @@
             pltpu.VMEM((2, 8, 128), f32),
             pltpu.VMEM((2, 2, 8, 128), f32),
             pltpu.VMEM((2, 128, 128), f32),
+            pltpu.VMEM((4 * GROUP, 8, 128), f32),
             dma((4,)),
             dma((3,)),
             dma,
@@ -378,7 +382,7 @@
             dma((2, 2, 3)),
         ],
         compiler_params=pltpu.CompilerParams(
-            collective_id=0, has_side_effects=True, vmem_limit_bytes=32 << 20
+            collective_id=0, has_side_effects=True, vmem_limit_bytes=56 << 20
         ),
         cost_estimate=pl.CostEstimate(flops=10**8, bytes_accessed=2 << 20, transcendentals=0),
     )(*args)

time: 71.3 us -> 55 us (0.77)
  Pallas kernels: 63.2 us -> 52.1 us
  local copies, waits for them, and re-layouts: 7.05 us -> 2.14 us
    pallas_call x1, Pallas kernels: 63.2 us -> 52.1 us  [shards(): pl.pallas_call(kernel, out_shape=[jax.ShapeDtypeStruct((16, 8, 128), f32)...]
    unnamed x16 -> x4, local copies, waits for them, and re-layouts: 7.05 us -> 2.14 us
where the time goes in v2:
time: 55 us; the launch traced here: 54.9 us
  Pallas kernels  52.1 us (95%)
  local copies, waits for them, and re-layouts  2.14 us (4%)
  between operations  0.65 us (1%)
    pallas_call x1, Pallas kernels, shards(): pl.pallas_call(kernel, out_shape=[jax.ShapeDtypeStruct((16, 8, 128), f32)...  52.1 us
    unnamed x4, local copies, waits for them, and re-layouts  2.14 us

profile of v2, /device:TPU:1, one launch (start us, length us, event | category | flops | bytes accessed | tf_op | source)
XLA Modules:
  0.0 54.9 jit_solution(10773860977291644662)
XLA Ops:
  0.6 52.1 %shard_map.86 = (f32[16,8,128]{2,1,0:T(8,128)}, f32[16,8,128]{2,1,0:T(8,128)}) custom-call(f32[16,8,128]{2,1,0:T(8,128)} %upper.1, f32[16,8,128]{2,1,0:T(8,128)} %lower.1, f32[3,16,8,128]{3,2,1,0:T(8,128)} %velocity.1, f32[16,8,128]{2,1,0:T(8,128)} %diffusivity.1, f32[1,128,1024]{2,1,0:T(8,128)} %center.1, f32[1,128]{1,0:T(1,128)} %error.1, s32[1,128]{1,0:T(1,128)} %block.1), custom_call_target="tpu_custom_call" | custom-call | flops 100000000 | bytes 2097152 | tf_op jit(solution)/shard_map/pallas_call | solution.py:353
  52.7 0.0 copy-start
  52.7 1.5 %copy.11 = f32[16,8,128]{2,1,0:T(8,128)} copy(f32[16,8,128]{2,1,0:T(8,128)} %get-tuple-element.4) | data formatting | bytes 131072
  54.2 0.0 copy-done
  54.2 0.6 %copy.12 = f32[16,8,128]{2,1,0:T(8,128)} copy(f32[16,8,128]{2,1,0:T(8,128)S(1)} %copy-done) | data formatting | bytes 131072
Async XLA Ops:
  52.7 1.5 %copy-start = (f32[16,8,128]{2,1,0:T(8,128)S(1)}, f32[16,8,128]{2,1,0:T(8,128)}, u32[]{:S(2)}) copy-start(f32[16,8,128]{2,1,0:T(8,128)} %get-tuple-element.5) | copy-start | bytes 196612

commit v3 on v2

--- a/solution.py
+++ b/solution.py
@@ -8,17 +8,18 @@
 MESH = pl.DeviceIdType.MESH
 N_X, N_Y, N_Z = 16, 8, 4
 OWNERS = N_X * N_Y
-GROUP = 16
-GROUPS = OWNERS // GROUP
-ROWS = 17
+HALF = OWNERS // 2
+FAR = ((1, 16), (16, 32), (32, 48), (48, 64))
+NEAR = ((1, 16), (16, 32), (32, 48), (48, 60), (60, 64))
+ROWS = (17, 16)
 PITCH = 24
 UP, LO, VZ, VX, VY, DIFF = range(6)
 
 
 def peer(i, gx, gy):
-    along_x = ((gx >> 1) + i) & 7
+    along_y = ((gx >> 1) + i) & 7
     core = (gx ^ (i >> 3)) & 1
-    return along_x * 2 + core, (gy + (i >> 4)) & (N_Y - 1)
+    return along_y * 2 + core, (gy + 2 * (i >> 4)) & (N_Y - 1)
 
 
 def lane_of(shape):
@@ -54,8 +55,8 @@
     upper, lower, velocity, diffusivity, center, error, block,
     upper_out, lower_out,
     fields, coefs, stage, err_v, blk_v, msg, got, ceil_t, floor_t, flat,
-    zs, zr, xs, xr, ys, yr, turn, wide,
-    in_sem, c_sem, send_sem, recv_sem, face_send, face_recv,
+    zs, zr, xs, xr, ys, yr, turn, wide, relay, relayed,
+    in_sem, c_sem, send_sem, far_sem, near_sem, relay_sem, face_send, face_recv,
 ):
     gx, gy, gz = lax.axis_index("gx"), lax.axis_index("gy"), lax.axis_index("gz")
 
@@ -80,11 +81,12 @@
         pl.semaphore_signal(barrier, inc=1, device_id=(px, py, gz), device_id_type=MESH)
         return carry
 
-    lax.fori_loop(1, OWNERS, greet, 0)
-    for d in (1, N_Z - 1):
-        pl.semaphore_signal(
-            barrier, inc=1, device_id=(gx, gy, lax.rem(gz + d, N_Z)), device_id_type=MESH
-        )
+    mirror = (gx, gy ^ 1, gz)
+    sideways = (gx, (gy + jnp.where((gy & 1) == 0, N_Y - 1, 1)) & (N_Y - 1), gz)
+    others = [mirror, sideways] + [(gx, gy, (gz + d) & (N_Z - 1)) for d in (1, N_Z - 1)]
+    for dev in others:
+        pl.semaphore_signal(barrier, inc=1, device_id=dev, device_id_type=MESH)
+    lax.fori_loop(1, HALF, greet, 0)
 
     loads[0].wait()
     loads[1].wait()
@@ -106,6 +108,8 @@
         l = jnp.sum(jnp.where(picks[r], local + 1.0, 0.0), axis=1, keepdims=True) - 1.0
         meta = jnp.where(sensor == 2 * r, e, meta)
         meta = jnp.where(sensor == 2 * r + 1, l, meta)
+    swapped = jnp.where((dest & 1) == 0, pltpu.roll(meta, OWNERS - 1, 0), pltpu.roll(meta, 1, 0))
+    meta = jnp.where(sensor < 4, meta, pltpu.roll(swapped, 4, 1))
     msg[pl.ds(16, OWNERS, stride=PITCH), :] = meta
     pick = jnp.concatenate([jnp.where(p, 1.0, 0.0) for p in picks], axis=0).astype(jnp.bfloat16)
     loads[2].wait()
@@ -169,29 +173,34 @@
 
     fill_faces([fields[UP], fields[LO]], [fields[VZ], fields[VX], fields[VY]])
 
-    pl.semaphore_wait(barrier, OWNERS - 1 + 2)
+    pl.semaphore_wait(barrier, HALF - 1 + len(others))
 
     first = face_copies(0)
     for c in first:
         c.start()
 
-    def message(i):
+    def slot(px, py, row):
+        return pl.multiple_of((px * N_Y + py) * PITCH + row, 8)
+
+    def message(i, near, group):
         px, py = peer(i, gx, gy)
-        at = pl.multiple_of((px * N_Y + py) * PITCH, 8)
         return pltpu.make_async_remote_copy(
-            src_ref=msg.at[pl.ds(at, ROWS)],
-            dst_ref=got.at[i, pl.ds(0, ROWS)],
-            send_sem=send_sem,
-            recv_sem=recv_sem.at[i >> 4],
+            src_ref=msg.at[pl.ds(slot(px, py if near else py ^ 1, 0), ROWS[near])],
+            dst_ref=got.at[near * HALF + i, pl.ds(0, ROWS[near])],
+            send_sem=send_sem.at[near],
+            recv_sem=(near_sem if near else far_sem).at[group],
             device_id=(px, py, gz),
             device_id_type=MESH,
         )
 
-    def send(i, carry):
-        message(i).start()
-        return carry
-
-    lax.fori_loop(1, OWNERS, send, 0)
+    for near, groups in ((0, FAR), (1, NEAR)):
+        for group, (lo, hi) in enumerate(groups):
+
+            def send(i, carry):
+                message(i, near, group).start()
+                return carry
+
+            lax.fori_loop(lo, hi, send, 0)
 
     x_of = lax.broadcasted_iota(jnp.int32, (16, 8, 128), 1)
     y_of = lax.broadcasted_iota(jnp.int32, (16, 8, 128), 2)
@@ -282,38 +291,44 @@
             ceil_t[b] = t[0][b]
             floor_t[b] = t[1][b]
 
-    def spread(m, row):
+    def spread(m, row, near):
         for k in range(4):
-            wide[4 * m + k] = jnp.broadcast_to(row[:, k : k + 1], (8, 128))
+            lane = 4 * near + k
+            wide[4 * m + k] = jnp.broadcast_to(row[:, lane : lane + 1], (8, 128))
 
     def take(t, m, rows):
         for r in range(2):
             t = merge(t, rows(r), wide[4 * m + 2 * r], wide[4 * m + 2 * r + 1])
         return t
 
-    full = lambda v: jnp.full((8, 128), v, jnp.float32)
-    own = (gx * N_Y + gy) * PITCH
-    start = (tuple(full(jnp.inf) for _ in range(16)), tuple(full(-jnp.inf) for _ in range(16)))
-    spread(0, msg[pl.ds(pl.multiple_of(own + 16, 8), 8), :][0:1])
-    store(take(start, 0, lambda r: msg[pl.ds(pl.multiple_of(own + 8 * r, 8), 8), :]))
-
-    def await_group(g):
-        lo = max(g * GROUP, 1)
-        n = (g + 1) * GROUP - lo
-        for_all = pltpu.make_async_remote_copy(
-            src_ref=got.at[pl.ds(lo, n), pl.ds(0, ROWS)],
-            dst_ref=got.at[pl.ds(lo, n), pl.ds(0, ROWS)],
-            send_sem=send_sem,
-            recv_sem=recv_sem.at[g],
-            device_id=(gx, gy, gz),
+    def begin(near):
+        full = lambda v: jnp.full((8, 128), v, jnp.float32)
+        start = (tuple(full(jnp.inf) for _ in range(16)), tuple(full(-jnp.inf) for _ in range(16)))
+        py = gy if near else gy ^ 1
+        spread(0, msg[pl.ds(slot(gx, gy ^ 1, 16), 8), :][0:1], near)
+        store(take(start, 0, lambda r: msg[pl.ds(slot(gx, py, 8 * r), 8), :]))
+
+    def arrived(near, group):
+        lo, hi = (NEAR if near else FAR)[group]
+        block_of = got.at[pl.ds(near * HALF + lo, hi - lo), pl.ds(0, ROWS[near])]
+        return pltpu.make_async_remote_copy(
+            src_ref=block_of,
+            dst_ref=block_of,
+            send_sem=send_sem.at[near],
+            recv_sem=(near_sem if near else far_sem).at[group],
+            device_id=mirror,
             device_id_type=MESH,
         )
-        for_all.wait_recv()
+
+    def await_group(near, group):
+        lo, hi = (NEAR if near else FAR)[group]
+        n = hi - lo
+        arrived(near, group).wait_recv()
         for m in range(n):
-            spread(m, got[lo + m, 16:17, :])
+            spread(m, got[lo + m, 16:17, :], near)
 
         def one(m, t):
-            return take(t, m, lambda r: got[lo + m, 8 * r : 8 * r + 8, :])
+            return take(t, m, lambda r: got[near * HALF + lo + m, 8 * r : 8 * r + 8, :])
 
         def body(h, t):
             return one(2 * h + 1, one(2 * h, t))
@@ -321,7 +336,20 @@
         t = lax.fori_loop(0, n // 2, body, tables())
         store(one(n - 1, t) if n % 2 else t)
 
-    await_group(0)
+    begin(0)
+    for group in range(len(FAR)):
+        await_group(0, group)
+    relay[0] = ceil_t[...]
+    relay[1] = floor_t[...]
+    hand_over = pltpu.make_async_remote_copy(
+        src_ref=relay,
+        dst_ref=relayed,
+        send_sem=relay_sem.at[0],
+        recv_sem=relay_sem.at[1],
+        device_id=mirror,
+        device_id_type=MESH,
+    )
+    hand_over.start()
 
     for c in second:
         c.wait()
@@ -330,8 +358,13 @@
     fields[UP] = twice[0]
     fields[LO] = twice[1]
 
-    for g in range(1, GROUPS):
-        await_group(g)
+    begin(1)
+    for group in range(len(NEAR) - 1):
+        await_group(1, group)
+    hand_over.wait()
+    ceil_t[...] = jnp.minimum(ceil_t[...], relayed[0])
+    floor_t[...] = jnp.maximum(floor_t[...], relayed[1])
+    await_group(1, len(NEAR) - 1)
 
     for table, which, out in ((ceil_t, UP, upper_out), (floor_t, LO, lower_out)):
         rows = regroup([table[b] for b in range(16)])
@@ -340,11 +373,9 @@
         pick_of = jnp.minimum if which == UP else jnp.maximum
         out[...] = pick_of(fields[which], flat[...].reshape(16, 8, 128))
 
-    def sent(i, carry):
-        message(i).wait_send()
-        return carry
-
-    lax.fori_loop(1, OWNERS, sent, 0)
+    for near, groups in ((0, FAR), (1, NEAR)):
+        for group in range(len(groups)):
+            arrived(near, group).wait_send()
 
 
 def shards(*args):
@@ -373,11 +404,15 @@
             pltpu.VMEM((2, 8, 128), f32),
             pltpu.VMEM((2, 2, 8, 128), f32),
             pltpu.VMEM((2, 128, 128), f32),
-            pltpu.VMEM((4 * GROUP, 8, 128), f32),
+            pltpu.VMEM((64, 8, 128), f32),
+            pltpu.VMEM((2, 16, 8, 128), f32),
+            pltpu.VMEM((2, 16, 8, 128), f32),
             dma((4,)),
             dma((3,)),
-            dma,
-            dma((GROUPS,)),
+            dma((2,)),
+            dma((len(FAR),)),
+            dma((len(NEAR),)),
+            dma((2,)),
             dma((2, 2, 3)),
             dma((2, 2, 3)),
         ],

time: 55 us -> 46.2 us (0.84)
  Pallas kernels: 52.1 us -> 43.2 us
    pallas_call x1, Pallas kernels: 52.1 us -> 43.2 us  [shards(): pl.pallas_call(kernel, out_shape=[jax.ShapeDtypeStruct((16, 8, 128), f32)...]
where the time goes in v3:
time: 46.2 us; the launch traced here: 45.9 us
  Pallas kernels  43.2 us (94%)
  local copies, waits for them, and re-layouts  2.14 us (5%)
  between operations  0.65 us (1%)
    pallas_call x1, Pallas kernels, shards(): pl.pallas_call(kernel, out_shape=[jax.ShapeDtypeStruct((16, 8, 128), f32)...  43.2 us
    unnamed x4, local copies, waits for them, and re-layouts  2.14 us

profile of v3, /device:TPU:1, one launch (start us, length us, event | category | flops | bytes accessed | tf_op | source)
XLA Modules:
  0.0 45.9 jit_solution(16774136001416370969)
XLA Ops:
  0.6 43.2 %shard_map.86 = (f32[16,8,128]{2,1,0:T(8,128)}, f32[16,8,128]{2,1,0:T(8,128)}) custom-call(f32[16,8,128]{2,1,0:T(8,128)} %upper.1, f32[16,8,128]{2,1,0:T(8,128)} %lower.1, f32[3,16,8,128]{3,2,1,0:T(8,128)} %velocity.1, f32[16,8,128]{2,1,0:T(8,128)} %diffusivity.1, f32[1,128,1024]{2,1,0:T(8,128)} %center.1, f32[1,128]{1,0:T(1,128)} %error.1, s32[1,128]{1,0:T(1,128)} %block.1), custom_call_target="tpu_custom_call" | custom-call | flops 100000000 | bytes 2097152 | tf_op jit(solution)/shard_map/pallas_call | solution.py:384
  43.8 0.0 copy-start
  43.8 1.5 %copy.11 = f32[16,8,128]{2,1,0:T(8,128)} copy(f32[16,8,128]{2,1,0:T(8,128)} %get-tuple-element.4) | data formatting | bytes 131072
  45.3 0.0 copy-done
  45.3 0.6 %copy.12 = f32[16,8,128]{2,1,0:T(8,128)} copy(f32[16,8,128]{2,1,0:T(8,128)S(1)} %copy-done) | data formatting | bytes 131072
Async XLA Ops:
  43.8 1.5 %copy-start = (f32[16,8,128]{2,1,0:T(8,128)S(1)}, f32[16,8,128]{2,1,0:T(8,128)}, u32[]{:S(2)}) copy-start(f32[16,8,128]{2,1,0:T(8,128)} %get-tuple-element.5) | copy-start | bytes 196612

commit v4 on v3

--- a/solution.py
+++ b/solution.py
@@ -53,7 +53,7 @@
 
 def kernel(
     upper, lower, velocity, diffusivity, center, error, block,
-    upper_out, lower_out,
+    both_out,
     fields, coefs, stage, err_v, blk_v, msg, got, ceil_t, floor_t, flat,
     zs, zr, xs, xr, ys, yr, turn, wide, relay, relayed,
     in_sem, c_sem, send_sem, far_sem, near_sem, relay_sem, face_send, face_recv,
@@ -366,7 +366,7 @@
     floor_t[...] = jnp.maximum(floor_t[...], relayed[1])
     await_group(1, len(NEAR) - 1)
 
-    for table, which, out in ((ceil_t, UP, upper_out), (floor_t, LO, lower_out)):
+    for table, which, out in ((ceil_t, UP, both_out.at[0]), (floor_t, LO, both_out.at[1])):
         rows = regroup([table[b] for b in range(16)])
         for g in range(16):
             flat[pl.ds(g, 8, stride=16), :] = rows[g]
@@ -381,11 +381,11 @@
 def shards(*args):
     f32 = jnp.float32
     dma = pltpu.SemaphoreType.DMA
-    return pl.pallas_call(
+    both = pl.pallas_call(
         kernel,
-        out_shape=[jax.ShapeDtypeStruct((16, 8, 128), f32)] * 2,
+        out_shape=pltpu.VMEM((2, 16, 8, 128), f32),
         in_specs=[pl.BlockSpec(memory_space=pl.ANY)] * 7,
-        out_specs=[pl.BlockSpec(memory_space=pltpu.VMEM)] * 2,
+        out_specs=pl.BlockSpec(memory_space=pltpu.VMEM),
         scratch_shapes=[
             pltpu.VMEM((6, 16, 8, 128), f32),
             pltpu.VMEM((7, 16, 8, 128), f32),
@@ -417,10 +417,11 @@
             dma((2, 2, 3)),
         ],
         compiler_params=pltpu.CompilerParams(
-            collective_id=0, has_side_effects=True, vmem_limit_bytes=56 << 20
+            collective_id=0, has_side_effects=True, vmem_limit_bytes=32 << 20
         ),
         cost_estimate=pl.CostEstimate(flops=10**8, bytes_accessed=2 << 20, transcendentals=0),
-    )(*args)
+    )(*[pltpu.with_memory_space_constraint(a, pltpu.HBM) for a in args])
+    return both[0], both[1]
 
 
 def solution(mesh):

time: 46.2 us -> 44 us (0.952)
  local copies, waits for them, and re-layouts: 2.14 us -> 0.66 us
  Pallas kernels: 43.2 us -> 42.5 us
    unnamed x4 -> x0, local copies, waits for them, and re-layouts: 2.14 us -> none
    squeeze x0 -> x1, local copies, waits for them, and re-layouts: none -> 0.66 us  [shards(): return (both[0], both[1])]
    pallas_call x1, Pallas kernels: 43.2 us -> 42.5 us  [shards(): pl.pallas_call(kernel, out_shape=pltpu.VMEM((2, 16, 8, 128), f32), in_spe...]
where the time goes in v4:
time: 44 us; the launch traced here: 43.8 us
  Pallas kernels  42.5 us (97%)
  local copies, waits for them, and re-layouts  0.66 us (2%)
  between operations  0.64 us (1%)
    pallas_call x1, Pallas kernels, shards(): pl.pallas_call(kernel, out_shape=pltpu.VMEM((2, 16, 8, 128), f32), in_spe...  42.5 us

profile of v4, /device:TPU:1, one launch (start us, length us, event | category | flops | bytes accessed | tf_op | source)
XLA Modules:
  0.0 43.8 jit_solution(11372918056115836599)
XLA Ops:
  0.6 42.5 %shard_map.86 = f32[2,16,8,128]{3,2,1,0:T(8,128)S(1)} custom-call(f32[16,8,128]{2,1,0:T(8,128)} %upper.1, f32[16,8,128]{2,1,0:T(8,128)} %lower.1, f32[3,16,8,128]{3,2,1,0:T(8,128)} %velocity.1, f32[16,8,128]{2,1,0:T(8,128)} %diffusivity.1, f32[1,128,1024]{2,1,0:T(8,128)} %center.1, f32[1,128]{1,0:T(1,128)} %error.1, s32[1,128]{1,0:T(1,128)} %block.1), custom_call_target="tpu_custom_call" | custom-call | flops 100000000 | bytes 2097152 | tf_op jit(solution)/shard_map/pallas_call | solution.py:384
  43.2 0.7 %slice_bitcast_fusion = (f32[16,8,128]{2,1,0:T(8,128)}, f32[16,8,128]{2,1,0:T(8,128)}) fusion(f32[2,16,8,128]{3,2,1,0:T(8,128)S(1)} %shard_map.86), kind=kLoop, calls=%fused_computation | loop fusion | bytes 262144 | tf_op jit(solution)/shard_map/squeeze | solution.py:424

commit v5 on v4

--- a/solution.py
+++ b/solution.py
@@ -11,7 +11,9 @@
 HALF = OWNERS // 2
 FAR = ((1, 16), (16, 32), (32, 48), (48, 64))
 NEAR = ((1, 16), (16, 32), (32, 48), (48, 60), (60, 64))
-ROWS = (17, 16)
+PART = ((8, 9), (0, 8))
+WHOLE = (0, 16)
+ROW = (8, 0)
 PITCH = 24
 UP, LO, VZ, VX, VY, DIFF = range(6)
 
@@ -54,9 +56,9 @@
 def kernel(
     upper, lower, velocity, diffusivity, center, error, block,
     both_out,
-    fields, coefs, stage, err_v, blk_v, msg, got, ceil_t, floor_t, flat,
+    fields, coefs, stage, err_v, blk_v, msg, got, tabs, flat,
     zs, zr, xs, xr, ys, yr, turn, wide, relay, relayed,
-    in_sem, c_sem, send_sem, far_sem, near_sem, relay_sem, face_send, face_recv,
+    in_sem, c_sem, send_sem, arrive_sem, relay_sem, face_send, face_recv, answer_sem,
 ):
     gx, gy, gz = lax.axis_index("gx"), lax.axis_index("gy"), lax.axis_index("gz")
 
@@ -81,12 +83,28 @@
         pl.semaphore_signal(barrier, inc=1, device_id=(px, py, gz), device_id_type=MESH)
         return carry
 
+    first_half = (gy & 1) == 0
     mirror = (gx, gy ^ 1, gz)
-    sideways = (gx, (gy + jnp.where((gy & 1) == 0, N_Y - 1, 1)) & (N_Y - 1), gz)
-    others = [mirror, sideways] + [(gx, gy, (gz + d) & (N_Z - 1)) for d in (1, N_Z - 1)]
-    for dev in others:
-        pl.semaphore_signal(barrier, inc=1, device_id=dev, device_id_type=MESH)
+    sideways = (gx, (gy + jnp.where(first_half, N_Y - 1, 1)) & (N_Y - 1), gz)
+    above, below = (gx, gy, (gz + 1) & (N_Z - 1)), (gx, gy, (gz + N_Z - 1) & (N_Z - 1))
+    last = gz == N_Z - 1
+    bottom = gz == 0
+    greets = [(first_half, mirror), (first_half, sideways), (gz < N_Z - 1, above), (bottom, below)]
+    answers = [
+        (jnp.logical_not(first_half), mirror, 0),
+        (jnp.logical_not(first_half), sideways, 1),
+        (gz > 0, below, 2),
+        (last, above, 3),
+    ]
+
+    def tell(when, sem, dev):
+        @pl.when(when)
+        def _():
+            pl.semaphore_signal(sem, inc=1, device_id=dev, device_id_type=MESH)
+
     lax.fori_loop(1, HALF, greet, 0)
+    for when, dev in greets:
+        tell(when, barrier, dev)
 
     loads[0].wait()
     loads[1].wait()
@@ -122,8 +140,9 @@
         out = jnp.dot(pick, part_a, preferred_element_type=jnp.float32)
         out += jnp.dot(pick, part_b, preferred_element_type=jnp.float32)
         out += jnp.dot(pick, part_c, preferred_element_type=jnp.float32)
-        msg[pl.ds(j, OWNERS, stride=PITCH), :] = out[:OWNERS]
-        msg[pl.ds(8 + j, OWNERS, stride=PITCH), :] = out[OWNERS:]
+        at = ROW[j // 4] + j % 4
+        msg[pl.ds(at, OWNERS, stride=PITCH), :] = out[:OWNERS]
+        msg[pl.ds(at + 4, OWNERS, stride=PITCH), :] = out[OWNERS:]
 
     for c in field_loads:
         c.wait()
@@ -173,34 +192,55 @@
 
     fill_faces([fields[UP], fields[LO]], [fields[VZ], fields[VX], fields[VY]])
 
-    pl.semaphore_wait(barrier, HALF - 1 + len(others))
+    greeted = sum(jnp.where(when, 1, 0) for when, _, _ in answers)
+    pl.semaphore_wait(barrier, HALF - 1 + greeted)
+    for when, dev, k in answers:
+        tell(when, answer_sem.at[k], dev)
+
+    def slot(px, py, row):
+        return pl.multiple_of((px * N_Y + py) * PITCH + row, 8)
+
+    def groups_of(phase):
+        return NEAR if phase == 2 else FAR
+
+    def rows_of(phase):
+        return WHOLE if phase == 2 else PART[phase]
+
+    def message(i, phase, group):
+        px, py = peer(i, gx, gy)
+        near = phase // 2
+        row, rows = rows_of(phase)
+        return pltpu.make_async_remote_copy(
+            src_ref=msg.at[pl.ds(slot(px, py if near else py ^ 1, row), rows)],
+            dst_ref=got.at[near * HALF + i, pl.ds(row, rows)],
+            send_sem=send_sem.at[phase],
+            recv_sem=arrive_sem.at[phase, group],
+            device_id=(px, py, gz),
+            device_id_type=MESH,
+        )
+
+    def send_groups(phase):
+        for group, (lo, hi) in enumerate(groups_of(phase)):
+
+            def body(i, carry):
+                message(i, phase, group).start()
+                return carry
+
+            lax.fori_loop(lo, hi, body, 0)
+
+    send_groups(0)
+    send_groups(1)
+
+    for k, (when, _) in enumerate(greets):
+
+        @pl.when(when)
+        def _():
+            pl.semaphore_wait(answer_sem.at[k], 1)
 
     first = face_copies(0)
     for c in first:
         c.start()
-
-    def slot(px, py, row):
-        return pl.multiple_of((px * N_Y + py) * PITCH + row, 8)
-
-    def message(i, near, group):
-        px, py = peer(i, gx, gy)
-        return pltpu.make_async_remote_copy(
-            src_ref=msg.at[pl.ds(slot(px, py if near else py ^ 1, 0), ROWS[near])],
-            dst_ref=got.at[near * HALF + i, pl.ds(0, ROWS[near])],
-            send_sem=send_sem.at[near],
-            recv_sem=(near_sem if near else far_sem).at[group],
-            device_id=(px, py, gz),
-            device_id_type=MESH,
-        )
-
-    for near, groups in ((0, FAR), (1, NEAR)):
-        for group, (lo, hi) in enumerate(groups):
-
-            def send(i, carry):
-                message(i, near, group).start()
-                return carry
-
-            lax.fori_loop(lo, hi, send, 0)
+    send_groups(2)
 
     x_of = lax.broadcasted_iota(jnp.int32, (16, 8, 128), 1)
     y_of = lax.broadcasted_iota(jnp.int32, (16, 8, 128), 2)
@@ -248,6 +288,93 @@
             sides.append(turn[d].T)
         return sides
 
+    upper_rows = lax.broadcasted_iota(jnp.int32, (8, 128), 0) < 4
+    full = lambda v: jnp.full((8, 128), v, jnp.float32)
+    nothing = (full(jnp.inf), full(-jnp.inf))
+    pick_of = (jnp.minimum, jnp.maximum)
+
+    def tables(part):
+        return tuple(tuple(tabs[part, kind, b] for b in range(16)) for kind in range(2))
+
+    def store(part, t):
+        for kind in range(2):
+            for b in range(16):
+                tabs[part, kind, b] = t[kind][b]
+
+    def spread(m, row, near):
+        for k in range(2):
+            a, b = (
+                jnp.broadcast_to(row[:, lane : lane + 1], (8, 128))
+                for lane in (4 * near + k, 4 * near + k + 2)
+            )
+            wide[2 * m + k] = jnp.where(upper_rows, a, b)
+
+    def begin(near):
+        py = gy if near else gy ^ 1
+        spread(0, msg[pl.ds(slot(gx, gy ^ 1, 16), 8), :][0:1], near)
+        start = tuple((nothing[kind],) * 16 for kind in range(2))
+        for part in range(2):
+            store(part, merge(start, msg[pl.ds(slot(gx, py, ROW[part]), 8), :], wide[0], wide[1]))
+
+    def arrived(phase, group):
+        lo, hi = groups_of(phase)[group]
+        row, rows = rows_of(phase)
+        block_of = got.at[pl.ds(phase // 2 * HALF + lo, hi - lo), pl.ds(row, rows)]
+        return pltpu.make_async_remote_copy(
+            src_ref=block_of,
+            dst_ref=block_of,
+            send_sem=send_sem.at[phase],
+            recv_sem=arrive_sem.at[phase, group],
+            device_id=mirror,
+            device_id_type=MESH,
+        )
+
+    def await_group(phase, group):
+        near = phase // 2
+        lo, hi = groups_of(phase)[group]
+        n = hi - lo
+        arrived(phase, group).wait_recv()
+        for m in range(n):
+            spread(m, got[lo + m, 16:17, :], near)
+        for part in (0, 1) if near else (phase,):
+
+            def one(m, t):
+                rows = got[near * HALF + lo + m, ROW[part] : ROW[part] + 8, :]
+                return merge(t, rows, wide[2 * m], wide[2 * m + 1])
+
+            def body(h, t):
+                return one(2 * h + 1, one(2 * h, t))
+
+            t = lax.fori_loop(0, n // 2, body, tables(part))
+            store(part, one(n - 1, t) if n % 2 else t)
+
+    def folded(part, kind, b):
+        t = tabs[part, kind, b]
+        return pick_of[kind](t, pltpu.roll(t, 4, 0))
+
+    def hand_over(part):
+        return pltpu.make_async_remote_copy(
+            src_ref=relay.at[part],
+            dst_ref=relayed.at[part],
+            send_sem=relay_sem.at[0, part],
+            recv_sem=relay_sem.at[1, part],
+            device_id=mirror,
+            device_id_type=MESH,
+        )
+
+    def far_part(part):
+        for group in range(len(FAR)):
+            await_group(part, group)
+        for kind in range(2):
+            for b in range(8):
+                relay[part, kind, b] = jnp.where(
+                    upper_rows, folded(part, kind, b), folded(part, kind, b + 8)
+                )
+        hand_over(part).start()
+
+    begin(0)
+    far_part(0)
+
     for c in first:
         c.wait()
     turned = turn_faces(0)
@@ -280,76 +407,7 @@
     for c in second:
         c.start()
 
-    def tables():
-        return (
-            tuple(ceil_t[b] for b in range(16)),
-            tuple(floor_t[b] for b in range(16)),
-        )
-
-    def store(t):
-        for b in range(16):
-            ceil_t[b] = t[0][b]
-            floor_t[b] = t[1][b]
-
-    def spread(m, row, near):
-        for k in range(4):
-            lane = 4 * near + k
-            wide[4 * m + k] = jnp.broadcast_to(row[:, lane : lane + 1], (8, 128))
-
-    def take(t, m, rows):
-        for r in range(2):
-            t = merge(t, rows(r), wide[4 * m + 2 * r], wide[4 * m + 2 * r + 1])
-        return t
-
-    def begin(near):
-        full = lambda v: jnp.full((8, 128), v, jnp.float32)
-        start = (tuple(full(jnp.inf) for _ in range(16)), tuple(full(-jnp.inf) for _ in range(16)))
-        py = gy if near else gy ^ 1
-        spread(0, msg[pl.ds(slot(gx, gy ^ 1, 16), 8), :][0:1], near)
-        store(take(start, 0, lambda r: msg[pl.ds(slot(gx, py, 8 * r), 8), :]))
-
-    def arrived(near, group):
-        lo, hi = (NEAR if near else FAR)[group]
-        block_of = got.at[pl.ds(near * HALF + lo, hi - lo), pl.ds(0, ROWS[near])]
-        return pltpu.make_async_remote_copy(
-            src_ref=block_of,
-            dst_ref=block_of,
-            send_sem=send_sem.at[near],
-            recv_sem=(near_sem if near else far_sem).at[group],
-            device_id=mirror,
-            device_id_type=MESH,
-        )
-
-    def await_group(near, group):
-        lo, hi = (NEAR if near else FAR)[group]
-        n = hi - lo
-        arrived(near, group).wait_recv()
-        for m in range(n):
-            spread(m, got[lo + m, 16:17, :], near)
-
-        def one(m, t):
-            return take(t, m, lambda r: got[near * HALF + lo + m, 8 * r : 8 * r + 8, :])
-
-        def body(h, t):
-            return one(2 * h + 1, one(2 * h, t))
-
-        t = lax.fori_loop(0, n // 2, body, tables())
-        store(one(n - 1, t) if n % 2 else t)
-
-    begin(0)
-    for group in range(len(FAR)):
-        await_group(0, group)
-    relay[0] = ceil_t[...]
-    relay[1] = floor_t[...]
-    hand_over = pltpu.make_async_remote_copy(
-        src_ref=relay,
-        dst_ref=relayed,
-        send_sem=relay_sem.at[0],
-        recv_sem=relay_sem.at[1],
-        device_id=mirror,
-        device_id_type=MESH,
-    )
-    hand_over.start()
+    far_part(1)
 
     for c in second:
         c.wait()
@@ -360,22 +418,31 @@
 
     begin(1)
     for group in range(len(NEAR) - 1):
-        await_group(1, group)
-    hand_over.wait()
-    ceil_t[...] = jnp.minimum(ceil_t[...], relayed[0])
-    floor_t[...] = jnp.maximum(floor_t[...], relayed[1])
-    await_group(1, len(NEAR) - 1)
-
-    for table, which, out in ((ceil_t, UP, both_out.at[0]), (floor_t, LO, both_out.at[1])):
-        rows = regroup([table[b] for b in range(16)])
+        await_group(2, group)
+    for part in range(2):
+        hand_over(part).wait_recv()
+        for kind in range(2):
+            for b in range(8):
+                came = relayed[part, kind, b]
+                for block_at, where in ((b, upper_rows), (b + 8, jnp.logical_not(upper_rows))):
+                    tabs[part, kind, block_at] = pick_of[kind](
+                        tabs[part, kind, block_at], jnp.where(where, came, nothing[kind])
+                    )
+    await_group(2, len(NEAR) - 1)
+
+    for kind, (which, out) in enumerate(((UP, both_out.at[0]), (LO, both_out.at[1]))):
+        rows = regroup(
+            [jnp.where(upper_rows, folded(0, kind, b), folded(1, kind, b)) for b in range(16)]
+        )
         for g in range(16):
             flat[pl.ds(g, 8, stride=16), :] = rows[g]
-        pick_of = jnp.minimum if which == UP else jnp.maximum
-        out[...] = pick_of(fields[which], flat[...].reshape(16, 8, 128))
-
-    for near, groups in ((0, FAR), (1, NEAR)):
-        for group in range(len(groups)):
-            arrived(near, group).wait_send()
+        out[...] = pick_of[kind](fields[which], flat[...].reshape(16, 8, 128))
+
+    for phase in range(3):
+        for group in range(len(groups_of(phase))):
+            arrived(phase, group).wait_send()
+    for part in range(2):
+        hand_over(part).wait_send()
 
 
 def shards(*args):
@@ -394,8 +461,7 @@
             pltpu.VMEM((1, 128), jnp.int32),
             pltpu.VMEM((OWNERS * PITCH, 128), f32),
             pltpu.VMEM((OWNERS, PITCH, 128), f32),
-            pltpu.VMEM((16, 8, 128), f32),
-            pltpu.VMEM((16, 8, 128), f32),
+            pltpu.VMEM((2, 2, 16, 8, 128), f32),
             pltpu.VMEM((128, 128), f32),
             pltpu.VMEM((2, 24, 128), f32),
             pltpu.VMEM((2, 2, 24, 128), f32),
@@ -405,16 +471,16 @@
             pltpu.VMEM((2, 2, 8, 128), f32),
             pltpu.VMEM((2, 128, 128), f32),
             pltpu.VMEM((64, 8, 128), f32),
-            pltpu.VMEM((2, 16, 8, 128), f32),
-            pltpu.VMEM((2, 16, 8, 128), f32),
+            pltpu.VMEM((2, 2, 8, 8, 128), f32),
+            pltpu.VMEM((2, 2, 8, 8, 128), f32),
             dma((4,)),
             dma((3,)),
-            dma((2,)),
-            dma((len(FAR),)),
-            dma((len(NEAR),)),
-            dma((2,)),
+            dma((3,)),
+            dma((3, len(NEAR))),
+            dma((2, 2)),
             dma((2, 2, 3)),
             dma((2, 2, 3)),
+            pltpu.SemaphoreType.REGULAR((4,)),
         ],
         compiler_params=pltpu.CompilerParams(
             collective_id=0, has_side_effects=True, vmem_limit_bytes=32 << 20

time: 44 us -> 43.2 us (0.982)
  Pallas kernels: 42.5 us -> 41.8 us
    pallas_call x1, Pallas kernels: 42.5 us -> 41.8 us  [shards(): pl.pallas_call(kernel, out_shape=pltpu.VMEM((2, 16, 8, 128), f32), in_spe...]
where the time goes in v5:
time: 43.2 us; the launch traced here: 43.1 us
  Pallas kernels  41.8 us (97%)
  local copies, waits for them, and re-layouts  0.66 us (2%)
  between operations  0.64 us (1%)
    pallas_call x1, Pallas kernels, shards(): pl.pallas_call(kernel, out_shape=pltpu.VMEM((2, 16, 8, 128), f32), in_spe...  41.8 us

profile of v5, /device:TPU:1, one launch (start us, length us, event | category | flops | bytes accessed | tf_op | source)
XLA Modules:
  0.0 43.1 jit_solution(2133672220397191585)
XLA Ops:
  0.6 41.8 %shard_map.86 = f32[2,16,8,128]{3,2,1,0:T(8,128)S(1)} custom-call(f32[16,8,128]{2,1,0:T(8,128)} %upper.1, f32[16,8,128]{2,1,0:T(8,128)} %lower.1, f32[3,16,8,128]{3,2,1,0:T(8,128)} %velocity.1, f32[16,8,128]{2,1,0:T(8,128)} %diffusivity.1, f32[1,128,1024]{2,1,0:T(8,128)} %center.1, f32[1,128]{1,0:T(1,128)} %error.1, s32[1,128]{1,0:T(1,128)} %block.1), custom_call_target="tpu_custom_call" | custom-call | flops 100000000 | bytes 2097152 | tf_op jit(solution)/shard_map/pallas_call | solution.py:451
  42.5 0.7 %slice_bitcast_fusion = (f32[16,8,128]{2,1,0:T(8,128)}, f32[16,8,128]{2,1,0:T(8,128)}) fusion(f32[2,16,8,128]{3,2,1,0:T(8,128)S(1)} %shard_map.86), kind=kLoop, calls=%fused_computation | loop fusion | bytes 262144 | tf_op jit(solution)/shard_map/squeeze | solution.py:490

commit v6 on v5

--- a/solution.py
+++ b/solution.py
@@ -14,6 +14,7 @@
 PART = ((8, 9), (0, 8))
 WHOLE = (0, 16)
 ROW = (8, 0)
+STEP_AFTER = 3
 PITCH = 24
 UP, LO, VZ, VX, VY, DIFF = range(6)
 
@@ -58,7 +59,7 @@
     both_out,
     fields, coefs, stage, err_v, blk_v, msg, got, tabs, flat,
     zs, zr, xs, xr, ys, yr, turn, wide, relay, relayed,
-    in_sem, c_sem, send_sem, arrive_sem, relay_sem, face_send, face_recv, answer_sem,
+    in_sem, c_sem, send_sem, arrive_sem, relay_sem, face_send, face_recv, answer_sem, row_sem,
 ):
     gx, gy, gz = lax.axis_index("gx"), lax.axis_index("gy"), lax.axis_index("gz")
 
@@ -78,11 +79,6 @@
 
     barrier = pltpu.get_barrier_semaphore()
 
-    def greet(i, carry):
-        px, py = peer(i, gx, gy)
-        pl.semaphore_signal(barrier, inc=1, device_id=(px, py, gz), device_id_type=MESH)
-        return carry
-
     first_half = (gy & 1) == 0
     mirror = (gx, gy ^ 1, gz)
     sideways = (gx, (gy + jnp.where(first_half, N_Y - 1, 1)) & (N_Y - 1), gz)
@@ -102,7 +98,12 @@
         def _():
             pl.semaphore_signal(sem, inc=1, device_id=dev, device_id_type=MESH)
 
-    lax.fori_loop(1, HALF, greet, 0)
+    same_y = [8 * k for k in range(1, 8)]
+    along_y = list(range(1, 8))
+    beside = ((gx + jnp.where((gx & 1) == 0, N_X - 1, 1)) & (N_X - 1), gy)
+    near_by = [peer(i, gx, gy) for i in same_y + along_y] + [beside]
+    for dev in near_by:
+        pl.semaphore_signal(barrier, inc=1, device_id=dev + (gz,), device_id_type=MESH)
     for when, dev in greets:
         tell(when, barrier, dev)
 
@@ -193,7 +194,11 @@
     fill_faces([fields[UP], fields[LO]], [fields[VZ], fields[VX], fields[VY]])
 
     greeted = sum(jnp.where(when, 1, 0) for when, _, _ in answers)
-    pl.semaphore_wait(barrier, HALF - 1 + greeted)
+    pl.semaphore_wait(barrier, len(near_by) + greeted)
+    for i in along_y:
+        pl.semaphore_signal(
+            row_sem.at[8 - i], inc=1, device_id=peer(i, gx, gy) + (gz,), device_id_type=MESH
+        )
     for when, dev, k in answers:
         tell(when, answer_sem.at[k], dev)
 
@@ -219,8 +224,9 @@
             device_id_type=MESH,
         )
 
-    def send_groups(phase):
-        for group, (lo, hi) in enumerate(groups_of(phase)):
+    def send_groups(phase, groups):
+        for group in groups:
+            lo, hi = groups_of(phase)[group]
 
             def body(i, carry):
                 message(i, phase, group).start()
@@ -228,8 +234,20 @@
 
             lax.fori_loop(lo, hi, body, 0)
 
-    send_groups(0)
-    send_groups(1)
+    def send_from(first, step, count):
+        def body(k, carry):
+            i = first + step * k
+            message(i, 0, i >> 4).start()
+            return carry
+
+        lax.fori_loop(0, count, body, 0)
+
+    send_from(1, 1, 7)
+    send_from(8, 8, 7)
+    for dy in (1, 7, 2, 6, 3, 5, 4):
+        pl.semaphore_wait(row_sem.at[dy], 1)
+        send_from(8 + dy, 8, 7)
+    send_groups(1, range(len(FAR)))
 
     for k, (when, _) in enumerate(greets):
 
@@ -240,7 +258,7 @@
     first = face_copies(0)
     for c in first:
         c.start()
-    send_groups(2)
+    send_groups(2, (0, 1))
 
     x_of = lax.broadcasted_iota(jnp.int32, (16, 8, 128), 1)
     y_of = lax.broadcasted_iota(jnp.int32, (16, 8, 128), 2)
@@ -406,8 +424,13 @@
     second = face_copies(1)
     for c in second:
         c.start()
+    send_groups(2, (2, 3, 4))
 
     far_part(1)
+
+    begin(1)
+    for group in range(STEP_AFTER):
+        await_group(2, group)
 
     for c in second:
         c.wait()
@@ -416,8 +439,7 @@
     fields[UP] = twice[0]
     fields[LO] = twice[1]
 
-    begin(1)
-    for group in range(len(NEAR) - 1):
+    for group in range(STEP_AFTER, len(NEAR) - 1):
         await_group(2, group)
     for part in range(2):
         hand_over(part).wait_recv()
@@ -481,6 +503,7 @@
             dma((2, 2, 3)),
             dma((2, 2, 3)),
             pltpu.SemaphoreType.REGULAR((4,)),
+            pltpu.SemaphoreType.REGULAR((8,)),
         ],
         compiler_params=pltpu.CompilerParams(
             collective_id=0, has_side_effects=True, vmem_limit_bytes=32 << 20

time: 43.2 us -> 41 us (0.949)
  Pallas kernels: 41.8 us -> 39.6 us
    pallas_call x1, Pallas kernels: 41.8 us -> 39.6 us  [shards(): pl.pallas_call(kernel, out_shape=pltpu.VMEM((2, 16, 8, 128), f32), in_spe...]
where the time goes in v6:
time: 41 us; the launch traced here: 40.9 us
  Pallas kernels  39.6 us (97%)
  local copies, waits for them, and re-layouts  0.66 us (2%)
  between operations  0.64 us (2%)
    pallas_call x1, Pallas kernels, shards(): pl.pallas_call(kernel, out_shape=pltpu.VMEM((2, 16, 8, 128), f32), in_spe...  39.6 us

profile of v6, /device:TPU:1, one launch (start us, length us, event | category | flops | bytes accessed | tf_op | source)
XLA Modules:
  0.0 40.9 jit_solution(14680045797269399951)
XLA Ops:
  0.6 39.6 %shard_map.86 = f32[2,16,8,128]{3,2,1,0:T(8,128)S(1)} custom-call(f32[16,8,128]{2,1,0:T(8,128)} %upper.1, f32[16,8,128]{2,1,0:T(8,128)} %lower.1, f32[3,16,8,128]{3,2,1,0:T(8,128)} %velocity.1, f32[16,8,128]{2,1,0:T(8,128)} %diffusivity.1, f32[1,128,1024]{2,1,0:T(8,128)} %center.1, f32[1,128]{1,0:T(1,128)} %error.1, s32[1,128]{1,0:T(1,128)} %block.1), custom_call_target="tpu_custom_call" | custom-call | flops 100000000 | bytes 2097152 | tf_op jit(solution)/shard_map/pallas_call | solution.py:473
  40.2 0.7 %slice_bitcast_fusion = (f32[16,8,128]{2,1,0:T(8,128)}, f32[16,8,128]{2,1,0:T(8,128)}) fusion(f32[2,16,8,128]{3,2,1,0:T(8,128)S(1)} %shard_map.86), kind=kLoop, calls=%fused_computation | loop fusion | bytes 262144 | tf_op jit(solution)/shard_map/squeeze | solution.py:513
